TPU v7x, 32 devices: a whole 2x2x4 slice. The times are simulated.
32 devices in a mesh: seq: 2 (over x), batch: 4 (over y, core), tp: 4 (over z).
Axes of the slice: x: 2, y: 2, z: 4, core: 2. Of those that a mesh axis runs over, the one named last changes fastest.
Arguments:
- tokens: bfloat16 [16, 1024, 768], P('batch', ('seq', 'tp')), may hold values from -6 to 6
- first_values: bfloat16 [16, 1024, 384], P('batch', ('seq', 'tp')), may hold values from -6 to 6
- segment_ids: int32 [16, 1024], P('batch'), may hold values from 0 to 7, as said below
- cotangent: bfloat16 [16, 1024, 768], P('batch', ('seq', 'tp')), may hold values from -6 to 6
- norm1_gain: float32 [768], replicated, may hold values from 0.25 to 1.75
- norm1_bias: float32 [768], replicated, may hold values from -1.75 to 1.75
- w_query: bfloat16 [768, 768], P(None, 'tp'), may hold values from -0.21875 to 0.21875
- b_query: float32 [768], P('tp'), may hold values from -3 to 3
- w_key: bfloat16 [768, 768], P(None, 'tp'), may hold values from -0.21875 to 0.21875
- w_value: bfloat16 [768, 384], replicated, may hold values from -0.21875 to 0.21875
- b_value: float32 [384], replicated, may hold values from -3 to 3
- w_out: bfloat16 [768, 768], P('tp'), may hold values from -0.875 to 0.875
- b_out: float32 [768], replicated, may hold values from -1.75 to 1.75
- norm2_gain: float32 [768], replicated, may hold values from 0.25 to 1.75
- norm2_bias: float32 [768], replicated, may hold values from -1.75 to 1.75
- w_up: bfloat16 [768, 3072], P(None, 'tp'), may hold values from -0.21875 to 0.21875
- b_up: float32 [3072], P('tp'), may hold values from -3 to 3
- w_down: bfloat16 [3072, 768], P('tp'), may hold values from -0.109375 to 0.109375
- b_down: float32 [768], replicated, may hold values from -1.75 to 1.75
Outputs:
- output: bfloat16 [16, 1024, 768], P('batch', ('seq', 'tp'))
- grad_tokens: float32 [16, 1024, 768], P('batch', ('seq', 'tp'))
- grad_first_values: bfloat16 [16, 1024, 384], P('batch', ('seq', 'tp'))
- grad_norm1_gain: float32 [768], replicated
- grad_norm1_bias: float32 [768], replicated
- grad_w_query: float32 [768, 768], P(None, 'tp')
- grad_b_query: float32 [768], P('tp')
- grad_w_key: float32 [768, 768], P(None, 'tp')
- grad_w_value: float32 [768, 384], replicated
- grad_b_value: float32 [384], replicated
- grad_w_out: float32 [768, 768], P('tp')
- grad_b_out: float32 [768], replicated
- grad_norm2_gain: float32 [768], replicated
- grad_norm2_bias: float32 [768], replicated
- grad_w_up: float32 [768, 3072], P(None, 'tp')
- grad_b_up: float32 [3072], P('tp')
- grad_w_down: float32 [3072, 768], P('tp')
- grad_b_down: float32 [768], replicated
Inputs may be any that keep to these rules, and one draw needn't show every extreme that they name: `segment_ids`: along each row the ids never fall. In each aligned block of 4 rows (the rows of one batch index) one row, drawn from the seed, is a single document of all 1024 tokens; the other rows are cut into documents at up to 7 positions, and end with id 7.
All inputs are finite; a program needn't handle non-finite values.
Results may differ from a plain program's by a relative error of at most 0.019.
Values may be sent and summed in bfloat16 or wider, within the bound.
A program may use at most 192 MiB of HBM per device.

v0:
```python
import math

import jax
import jax.numpy as jnp
from jax import lax
from jax.sharding import PartitionSpec as P

HEADS = 12
HEAD_DIM = 64


eps = 1e-05
block_cap = 256
far_below = -1e30


def from_behind(block, axis, distance):
    devices = range(lax.axis_size(axis))
    route = [((i - distance) % len(devices), i) for i in devices]
    return lax.ppermute(block, axis, route)


def layer_norm(values, norm_gain, norm_bias):
    average = jnp.mean(values, axis=-1, keepdims=True)
    centered = values - average
    inverse = lax.rsqrt(jnp.mean(centered * centered, axis=-1, keepdims=True) + eps)
    unit = centered * inverse
    return (unit * norm_gain + norm_bias, unit, inverse)


def norm_back(grad_result, unit, inverse, norm_gain):
    scaled = grad_result * norm_gain
    return inverse * (
        scaled
        - jnp.mean(scaled, axis=-1, keepdims=True)
        - unit * jnp.mean(scaled * unit, axis=-1, keepdims=True)
    )


def project(values, weight):
    return jnp.einsum("rtd,de->rte", values, weight, preferred_element_type=jnp.float32)


def project_back(grads, weight):
    return jnp.einsum("rte,de->rtd", grads, weight, preferred_element_type=jnp.float32)


def weight_grad(values, grads):
    return jnp.einsum("rtd,rte->de", values, grads, preferred_element_type=jnp.float32)


def column_sum(values):
    return jnp.sum(values, axis=(0, 1), dtype=jnp.float32)


def gelu_tanh(values):
    return jax.nn.gelu(values, approximate=True)


def over_key_blocks(arrays, key_first, state, step, limit):
    count = arrays[0].shape[1]
    width = math.gcd(count, block_cap)

    def one(index, carry):
        offset = index * width
        parts = tuple((lax.dynamic_slice_in_dim(item, offset, width, 1) for item in arrays))
        first_key = key_first + offset

        def taken(inner):
            return step(inner, parts, first_key, offset)

        def skipped(inner):
            return inner

        return lax.cond(first_key <= limit, taken, skipped, carry)

    return lax.fori_loop(0, count // width, one, state)


def on_device(
    tokens,
    first_values,
    segment_ids,
    cotangent,
    norm1_gain,
    norm1_bias,
    w_query,
    b_query,
    w_key,
    w_value,
    b_value,
    w_out,
    b_out,
    norm2_gain,
    norm2_bias,
    w_up,
    b_up,
    w_down,
    b_down,
):
    rows = tokens.shape[0]
    model_width = tokens.shape[2]
    tp_count = lax.axis_size("tp")
    seq_count = lax.axis_size("seq")
    local_len = tokens.shape[1] * tp_count
    heads = w_query.shape[1] // HEAD_DIM
    width_tp = heads * HEAD_DIM
    valf_all = w_value.shape[1]
    factor = HEAD_DIM ** (-0.5)
    seq_index = lax.axis_index("seq")
    head_first = lax.axis_index("tp") * heads
    is_fresh = head_first < HEADS // 2
    fresh_col = jnp.minimum(head_first * HEAD_DIM, valf_all - width_tp)
    reuse_col = jnp.maximum(head_first * HEAD_DIM - valf_all, 0)
    own_first = seq_index * local_len
    own_last = own_first + local_len - 1
    own_pos = own_first + jnp.arange(local_len, dtype=jnp.int32)
    own_seg = lax.dynamic_slice_in_dim(segment_ids, own_first, local_len, 1)

    def masked_scores(query4, key_part, query_pos, query_seg, key_first):
        width = key_part.shape[1]
        scores = (
            jnp.einsum("rqhc,rkhc->rhqk", query4, key_part, preferred_element_type=jnp.float32)
            * factor
        )
        key_seg = lax.dynamic_slice_in_dim(segment_ids, key_first, width, 1)
        key_pos = key_first + jnp.arange(width, dtype=jnp.int32)
        allowed = (query_seg[:, :, None] == key_seg[:, None, :]) & (
            key_pos[None, None, :] <= query_pos[None, :, None]
        )
        return (scores, allowed[:, None])

    resid = tokens.astype(jnp.float32)
    normed_one, unit_one, inverse_one = layer_norm(resid, norm1_gain, norm1_bias)
    rows_one, grad_rows, first_rows = (
        lax.all_gather(normed_one.astype(jnp.bfloat16), "tp", axis=1, tiled=True),
        lax.all_gather(cotangent, "tp", axis=1, tiled=True),
        lax.all_gather(first_values, "tp", axis=1, tiled=True),
    )
    query4 = (
        (project(rows_one, w_query) + b_query)
        .astype(jnp.bfloat16)
        .reshape(rows, local_len, heads, HEAD_DIM)
    )
    keys4 = project(rows_one, w_key).astype(jnp.bfloat16).reshape(rows, local_len, heads, HEAD_DIM)
    w_part = lax.dynamic_slice_in_dim(w_value, fresh_col, width_tp, 1)
    b_part = lax.dynamic_slice_in_dim(b_value, fresh_col, width_tp, 0)

    def fresh_side(normed_rows):
        return (project(normed_rows, w_part) + b_part).astype(jnp.bfloat16)

    def reuse_side(normed_rows):
        return lax.dynamic_slice_in_dim(first_rows, reuse_col, width_tp, 2)

    vals4 = lax.cond(is_fresh, fresh_side, reuse_side, rows_one).reshape(
        rows, local_len, heads, HEAD_DIM
    )

    def stats_step(carry, parts, key_first, offset):
        top, total = carry
        scores, allowed = masked_scores(query4, parts[0], own_pos, own_seg, key_first)
        masked = jnp.where(allowed, scores, far_below)
        new_top = jnp.maximum(top, jnp.max(masked, axis=3))
        weights = jnp.where(allowed, jnp.exp(masked - new_top[..., None]), 0.0)
        return (new_top, total * jnp.exp(top - new_top) + jnp.sum(weights, axis=3))

    start_top = jnp.full((rows, heads, local_len), far_below, jnp.float32)
    start_total = jnp.zeros((rows, heads, local_len), jnp.float32)
    top, total = over_key_blocks(
        (lax.all_gather(keys4, "seq", axis=1, tiled=True),),
        jnp.int32(0),
        (start_top, start_total),
        stats_step,
        own_last,
    )
    lse = top + jnp.log(total)

    def value_step(acc, parts, key_first, offset):
        scores, allowed = masked_scores(query4, parts[0], own_pos, own_seg, key_first)
        weights = jnp.where(allowed, jnp.exp(scores - lse[..., None]), 0.0).astype(jnp.bfloat16)
        return acc + jnp.einsum(
            "rhqk,rkhc->rqhc", weights, parts[1], preferred_element_type=jnp.float32
        )

    zeros_q = jnp.zeros((rows, local_len, heads, HEAD_DIM), jnp.float32)
    attended = over_key_blocks(
        (
            lax.all_gather(keys4, "seq", axis=1, tiled=True),
            lax.all_gather(vals4, "seq", axis=1, tiled=True),
        ),
        jnp.int32(0),
        zeros_q,
        value_step,
        own_last,
    )
    attended_low = attended.astype(jnp.bfloat16).reshape(rows, local_len, width_tp)
    attn_share = lax.psum_scatter(
        project(attended_low, w_out).astype(jnp.bfloat16), "tp", scatter_dimension=1, tiled=True
    ).astype(jnp.float32)
    middle = resid + attn_share + b_out
    normed_two, unit_two, inverse_two = layer_norm(middle, norm2_gain, norm2_bias)
    rows_two = lax.all_gather(normed_two.astype(jnp.bfloat16), "tp", axis=1, tiled=True)
    hidden_pre = project(rows_two, w_up) + b_up
    activated_full, gelu_pull = jax.vjp(gelu_tanh, hidden_pre)
    activated = activated_full.astype(jnp.bfloat16)
    mlp_share = lax.psum_scatter(
        project(activated, w_down).astype(jnp.bfloat16), "tp", scatter_dimension=1, tiled=True
    ).astype(jnp.float32)
    output = (middle + mlp_share + b_down).astype(jnp.bfloat16)
    grad_b_down = column_sum(grad_rows)
    grad_w_down = weight_grad(activated, grad_rows)
    grad_hidden = gelu_pull(project_back(grad_rows, w_down))[0].astype(jnp.bfloat16)
    grad_b_up = column_sum(grad_hidden)
    grad_w_up = weight_grad(rows_two, grad_hidden)
    back_two = lax.psum_scatter(
        project_back(grad_hidden, w_up).astype(jnp.bfloat16), "tp", scatter_dimension=1, tiled=True
    ).astype(jnp.float32)
    grad_gain_two = jnp.sum(back_two * unit_two, axis=(0, 1))
    grad_bias_two = jnp.sum(back_two, axis=(0, 1))
    grad_middle = cotangent.astype(jnp.float32) + norm_back(
        back_two, unit_two, inverse_two, norm2_gain
    )
    grad_mid_rows = lax.all_gather(grad_middle.astype(jnp.bfloat16), "tp", axis=1, tiled=True)
    grad_b_out = column_sum(grad_mid_rows)
    grad_w_out = weight_grad(attended_low, grad_mid_rows)
    grad_out4 = (
        project_back(grad_mid_rows, w_out)
        .astype(jnp.bfloat16)
        .reshape(rows, local_len, heads, HEAD_DIM)
    )
    delta = jnp.einsum("rqhc,rqhc->rhq", grad_out4.astype(jnp.float32), attended)

    def pair_terms(key_side, val_side, key_first, grad_query, grad_keys, grad_vals):

        def pair_step(carry, parts, first, offset):
            acc_query, acc_keys, acc_vals = carry
            key_part, val_part = parts
            width = key_part.shape[1]
            scores, allowed = masked_scores(query4, key_part, own_pos, own_seg, first)
            probs = jnp.where(allowed, jnp.exp(scores - lse[..., None]), 0.0)
            grad_val = jnp.einsum(
                "rhqk,rqhc->rkhc",
                probs.astype(jnp.bfloat16),
                grad_out4,
                preferred_element_type=jnp.float32,
            )
            grad_prob = jnp.einsum(
                "rqhc,rkhc->rhqk", grad_out4, val_part, preferred_element_type=jnp.float32
            )
            grad_score = (probs * (grad_prob - delta[..., None])).astype(jnp.bfloat16)
            acc_query = (
                acc_query
                + jnp.einsum(
                    "rhqk,rkhc->rqhc", grad_score, key_part, preferred_element_type=jnp.float32
                )
                * factor
            )
            grad_key = (
                jnp.einsum(
                    "rhqk,rqhc->rkhc", grad_score, query4, preferred_element_type=jnp.float32
                )
                * factor
            )
            acc_keys = lax.dynamic_update_slice_in_dim(
                acc_keys, lax.dynamic_slice_in_dim(acc_keys, offset, width, 1) + grad_key, offset, 1
            )
            acc_vals = lax.dynamic_update_slice_in_dim(
                acc_vals, lax.dynamic_slice_in_dim(acc_vals, offset, width, 1) + grad_val, offset, 1
            )
            return (acc_query, acc_keys, acc_vals)

        return over_key_blocks(
            (key_side, val_side), key_first, (grad_query, grad_keys, grad_vals), pair_step, own_last
        )

    def turn_keys(turn, carry):
        moving_keys, moving_vals, moving_gk, moving_gv, grad_query = carry
        anchor = (seq_index - turn) % seq_count
        grad_query, moving_gk, moving_gv = pair_terms(
            moving_keys, moving_vals, anchor * local_len, grad_query, moving_gk, moving_gv
        )
        moving_keys, moving_vals, moving_gk, moving_gv = (
            from_behind(moving_keys, "seq", 1),
            from_behind(moving_vals, "seq", 1),
            from_behind(moving_gk.astype(jnp.bfloat16), "seq", 1).astype(moving_gk.dtype),
            from_behind(moving_gv.astype(jnp.bfloat16), "seq", 1).astype(moving_gv.dtype),
        )
        return (moving_keys, moving_vals, moving_gk, moving_gv, grad_query)

    start_state = (keys4, vals4, zeros_q, zeros_q, zeros_q)
    final_state = lax.fori_loop(0, seq_count, turn_keys, start_state)
    grad_keys4, grad_vals4, grad_query4 = (final_state[2], final_state[3], final_state[4])
    grad_query = grad_query4.astype(jnp.bfloat16).reshape(rows, local_len, width_tp)
    grad_keys = grad_keys4.astype(jnp.bfloat16).reshape(rows, local_len, width_tp)
    grad_vals = grad_vals4.astype(jnp.bfloat16).reshape(rows, local_len, width_tp)

    def fresh_back(grad_flat):
        gw_full = lax.dynamic_update_slice_in_dim(
            jnp.zeros((model_width, valf_all), jnp.float32),
            weight_grad(rows_one, grad_flat),
            fresh_col,
            1,
        )
        gb_full = lax.dynamic_update_slice_in_dim(
            jnp.zeros((valf_all,), jnp.float32), column_sum(grad_flat), fresh_col, 0
        )
        back_value = project_back(grad_flat, w_part)
        reuse_full = jnp.zeros((rows, local_len, valf_all), jnp.float32)
        return (gw_full, gb_full, back_value, reuse_full)

    def reuse_back(grad_flat):
        gw_full = jnp.zeros((model_width, valf_all), jnp.float32)
        gb_full = jnp.zeros((valf_all,), jnp.float32)
        back_value = jnp.zeros((rows, local_len, model_width), jnp.float32)
        reuse_full = lax.dynamic_update_slice_in_dim(
            jnp.zeros((rows, local_len, valf_all), jnp.float32),
            grad_flat.astype(jnp.float32),
            reuse_col,
            2,
        )
        return (gw_full, gb_full, back_value, reuse_full)

    grad_w_value, grad_b_value, back_value, reuse_full = lax.cond(
        is_fresh, fresh_back, reuse_back, grad_vals
    )
    grad_b_query = column_sum(grad_query)
    grad_w_query = weight_grad(rows_one, grad_query)
    grad_w_key = weight_grad(rows_one, grad_keys)
    back_terms = project_back(grad_query, w_query) + project_back(grad_keys, w_key) + back_value
    back_one, reuse_sum = (
        lax.psum_scatter(
            back_terms.astype(jnp.bfloat16), "tp", scatter_dimension=1, tiled=True
        ).astype(jnp.float32),
        lax.psum_scatter(
            reuse_full.astype(jnp.bfloat16), "tp", scatter_dimension=1, tiled=True
        ).astype(jnp.float32),
    )
    grad_first_values = reuse_sum.astype(jnp.bfloat16)
    grad_gain_one = jnp.sum(back_one * unit_one, axis=(0, 1))
    grad_bias_one = jnp.sum(back_one, axis=(0, 1))
    grad_tokens = grad_middle + norm_back(back_one, unit_one, inverse_one, norm1_gain)
    summed = lax.psum(
        (
            grad_w_query,
            grad_w_key,
            grad_w_out,
            grad_w_up,
            grad_w_down,
            grad_b_query,
            grad_b_out,
            grad_b_up,
            grad_b_down,
        ),
        ("seq", "batch"),
    )
    norm_sums = lax.psum(
        (grad_gain_one, grad_bias_one, grad_gain_two, grad_bias_two, grad_w_value, grad_b_value),
        ("seq", "batch", "tp"),
    )
    return (
        output,
        grad_tokens,
        grad_first_values,
        norm_sums[0],
        norm_sums[1],
        summed[0],
        summed[5],
        summed[1],
        norm_sums[4],
        norm_sums[5],
        summed[2],
        summed[6],
        norm_sums[2],
        norm_sums[3],
        summed[3],
        summed[7],
        summed[4],
        summed[8],
    )


def solution(mesh):
    placed = (
        P("batch", ("seq", "tp"), None),
        P("batch", ("seq", "tp"), None),
        P("batch", None),
        P("batch", ("seq", "tp"), None),
        P(),
        P(),
        P(None, "tp"),
        P("tp"),
        P(None, "tp"),
        P(),
        P(),
        P("tp", None),
        P(),
        P(),
        P(),
        P(None, "tp"),
        P("tp"),
        P("tp", None),
        P(),
    )
    return jax.shard_map(
        on_device,
        mesh=mesh,
        in_specs=placed,
        out_specs=(
            P("batch", ("seq", "tp"), None),
            P("batch", ("seq", "tp"), None),
            P("batch", ("seq", "tp"), None),
            P(),
            P(),
            P(None, "tp"),
            P("tp"),
            P(None, "tp"),
            P(),
            P(),
            P("tp", None),
            P(),
            P(),
            P(),
            P(None, "tp"),
            P("tp"),
            P("tp", None),
            P(),
        ),
        check_vma=False,
    )
```

profile of v0, /device:TPU:1, one launch (start us, length us, event | category | flops | bytes accessed | tf_op | source)
XLA Modules:
  0.0 1229.7 jit_solution(16260476120367123979)
XLA Ops:
  12.7 64.6 %all-gather.8.cloned.1.call-done = bf16[4,512,768]{2,1,0:T(8,128)(2,1)} async-done(((bf16[4,128,768]{2,1,0:T(8,128)(2,1)}), bf16[4,512,768]{2,1,0:T(8,128)(2,1)}) %all-gather.8.cloned.1.call-update) | async-done | bytes 3145744 | tf_op jit(solution)/shard_map/all_gather | solution.py:136
  82.4 32.1 %all-gather.12.cloned.1.call-done = bf16[4,512,384]{1,2,0:T(8,128)(2,1)} async-done(((bf16[4,128,384]{1,2,0:T(8,128)(2,1)}), bf16[4,512,384]{1,2,0:T(8,128)(2,1)}) %all-gather.12.cloned.1.call-update) | async-done | bytes 1572880 | tf_op jit(solution)/shard_map/all_gather | solution.py:138
  124.6 18.5 %all-gather.10.cloned.1.call-done = bf16[4,1024,3,64]{1,3,2,0:T(8,128)(2,1)} async-done(((bf16[4,512,3,64]{1,3,2,0:T(8,128)(2,1)}), bf16[4,1024,3,64]{1,3,2,0:T(8,128)(2,1)}) %all-gather.10.cloned.1.call-update) | async-done | bytes 1572880 | tf_op jit(solution)/shard_map/all_gather | solution.py:188
  149.9 9.6 while.105
  159.5 12.0 all-gather.14.cloned.1.call-done
  172.9 18.5 %while.106 = (s32[]{:T(128)}, f32[4,512,3,64]{1,3,2,0:T(8,128)}, s32[]{:T(128)}, s32[4,512]{1,0:T(4,128)S(1)}, s32[4,1024]{1,0:T(4,128)S(1)}, /*index=5*/bf16[4,...) while((s32[]{:T(128)}, f32[4,512,3,64]{1,3,2,0:T(8,128)}, ...), condition=%wide.region_13.14_spmd.clone, body=%wide.region_10.13_spmd.clone.sunk | while | flops 410518272 | bytes 8837405 | solution.py:77
  196.9 78.6 %reduce-scatter.6.cloned.1.call-done = bf16[4,128,768]{2,1,0:T(8,128)(2,1)} async-done(((bf16[4,512,768]{2,1,0:T(8,128)(2,1)}), bf16[4,128,768]{2,1,0:T(8,128)(2,1)}) %reduce-scatter.6.cloned.1.call-update) | async-done | bytes 786448 | tf_op jit(solution)/shard_map/reduce_scatter | solution.py:197
  281.5 62.5 %all-gather.16.cloned.1.call-done = bf16[4,512,768]{2,1,0:T(8,128)(2,1)} async-done(((bf16[4,128,768]{2,1,0:T(8,128)(2,1)}), bf16[4,512,768]{2,1,0:T(8,128)(2,1)}) %all-gather.16.cloned.1.call-update) | async-done | bytes 3145744 | tf_op jit(solution)/shard_map/all_gather | solution.py:202
  351.5 56.2 %all-gather.18.cloned.1.call-done = bf16[4,512,768]{2,1,0:T(8,128)(2,1)} async-done(((bf16[4,128,768]{2,1,0:T(8,128)(2,1)}), bf16[4,512,768]{2,1,0:T(8,128)(2,1)}) %all-gather.18.cloned.1.call-update) | async-done | bytes 3145744 | tf_op jit(solution)/shard_map/all_gather | solution.py:137
  407.8 10.9 convert_reduce_fusion.2
  424.5 58.9 %reduce-scatter.10.cloned.1.call-done = bf16[4,128,768]{2,1,0:T(8,128)(2,1)} async-done(((bf16[4,512,768]{2,1,0:T(8,128)(2,1)}), bf16[4,128,768]{2,1,0:T(8,128)(2,1)}) %reduce-scatter.10.cloned.1.call-update) | async-done | bytes 786448 | tf_op jit(solution)/shard_map/reduce_scatter | solution.py:215
  489.4 63.5 %all-gather.20.cloned.1.call-done = bf16[4,512,768]{2,1,0:T(8,128)(2,1)} async-done(((bf16[4,128,768]{2,1,0:T(8,128)(2,1)}), bf16[4,512,768]{2,1,0:T(8,128)(2,1)}) %all-gather.20.cloned.1.call-update) | async-done | bytes 3145744 | tf_op jit(solution)/shard_map/all_gather | solution.py:223
  557.2 211.2 %while.108 = (s32[]{:T(128)}, bf16[4,512,3,64]{1,3,2,0:T(8,128)(2,1)}, bf16[4,512,3,64]{1,3,2,0:T(8,128)(2,1)}, f32[4,512,3,64]{1,3,2,0:T(8,128)}, f32[4,512,3,6...) while((s32[]{:T(128)}, ...), condition=%wide.region_26.27_spmd.clone, body=%wide.region_21.26_spmd.clone.sunk | while | flops 1027277568 | bytes 88247512 | solution.py:291
  563.6 27.1 %while.109 = (s32[]{:T(128)}, f32[4,512,3,64]{1,3,2,0:T(8,128)S(1)}, f32[4,512,3,64]{1,3,2,0:T(8,128)}, f32[4,512,3,64]{1,3,2,0:T(8,128)}, s32[]{:T(128)}, /*ind...) while((s32[]{:T(128)}, f32[4,512,3,64]{1,3,2,0:T(8,128)S(1)}, ...), condition=%wide.region_25.25_spmd, body=%wide.region_22.0_spmd.sunk | while | flops 1024917760 | bytes 56787544 | solution.py:77
  563.6 13.5 %conditional.14 = ((f32[4,512,3,64]{1,3,2,0:T(8,128)S(1)}, f32[4,512,3,64]{1,3,2,0:T(8,128)}, f32[4,512,3,64]{1,3,2,0:T(8,128)})) conditional(s32[]{:T(128)} %convert_element_type.377, (f32[4,512,3,64]{1,3,2,0:T(8,128)S(1)}, f32[4,512,3,64]{1,3,2,0:T(8,128)}, f32[4,512,3,64]{1,3,2,0:T(8,128)}) %tuple.226, (s32[4,512]{1,0:T(4,128)S(1)}, s32[]{:T(128)}, ...), branch_computations={%region_23.22_spmd, %region_24.23_spmd} | conditional | flops 1024917760 | bytes 56787212 | solution.py:75
  577.1 13.5 %conditional.14 = ((f32[4,512,3,64]{1,3,2,0:T(8,128)S(1)}, f32[4,512,3,64]{1,3,2,0:T(8,128)}, f32[4,512,3,64]{1,3,2,0:T(8,128)})) conditional(s32[]{:T(128)} %convert_element_type.377, (f32[4,512,3,64]{1,3,2,0:T(8,128)S(1)}, f32[4,512,3,64]{1,3,2,0:T(8,128)}, f32[4,512,3,64]{1,3,2,0:T(8,128)}) %tuple.226, (s32[4,512]{1,0:T(4,128)S(1)}, s32[]{:T(128)}, ...), branch_computations={%region_23.22_spmd, %region_24.23_spmd} | conditional | flops 1024917760 | bytes 56787212 | solution.py:75
  598.4 13.4 %collective-permute-done.2 = bf16[4,512,3,64]{1,3,2,0:T(8,128)(2,1)} collective-permute-done((bf16[4,512,3,64]{1,3,2,0:T(8,128)(2,1)}, bf16[4,512,3,64]{1,3,2,0:T(8,128)(2,1)}, u32[]{:S(2)}, u32[]{:S(2)}) %collective-permute-start.2) | collective-permute-done | bytes 786464 | tf_op jit(solution)/shard_map/while/body/eval_jaxpr/ppermute | solution.py:20
  614.3 14.4 %collective-permute-done.3 = bf16[4,512,3,64]{1,3,2,0:T(8,128)(2,1)} collective-permute-done((bf16[4,512,3,64]{1,3,2,0:T(8,128)(2,1)}, bf16[4,512,3,64]{1,3,2,0:T(8,128)(2,1)}, u32[]{:S(2)}, u32[]{:S(2)}) %collective-permute-start.3) | collective-permute-done | bytes 786464 | tf_op jit(solution)/shard_map/while/body/eval_jaxpr/ppermute | solution.py:20
  631.1 14.4 %collective-permute-done = bf16[4,512,3,64]{1,3,2,0:T(8,128)(2,1)} collective-permute-done((bf16[4,512,3,64]{1,3,2,0:T(8,128)(2,1)}, bf16[4,512,3,64]{1,3,2,0:T(8,128)(2,1)}, u32[]{:S(2)}, u32[]{:S(2)}) %collective-permute-start) | collective-permute-done | bytes 786464 | tf_op jit(solution)/shard_map/while/body/eval_jaxpr/ppermute | solution.py:20
  645.5 16.9 %collective-permute-done.1 = bf16[4,512,3,64]{1,3,2,0:T(8,128)(2,1)} collective-permute-done((bf16[4,512,3,64]{1,3,2,0:T(8,128)(2,1)}, bf16[4,512,3,64]{1,3,2,0:T(8,128)(2,1)}, u32[]{:S(2)}, u32[]{:S(2)}) %collective-permute-start.1) | collective-permute-done | bytes 786464 | tf_op jit(solution)/shard_map/while/body/eval_jaxpr/ppermute | solution.py:20
  673.0 28.3 %collective-permute-start.2 = (bf16[4,512,3,64]{1,3,2,0:T(8,128)(2,1)}, bf16[4,512,3,64]{1,3,2,0:T(8,128)(2,1)}, u32[]{:S(2)}, u32[]{:S(2)}) collective-permute-start(bf16[4,512,3,64]{1,3,2,0:T(8,128)(2,1)} %convert_element_type.373), channel_id=1, source_target_pairs={{16,0},{0,16},{17,1},{1,17},{18,2},{2,18},{19,3},{3,19},{20,4},{4,... | collective-permute-start | bytes 2359304 | tf_op jit(solution)/shard_map/while/body/eval_jaxpr/ppermute | solution.py:20
  705.2 12.7 %collective-permute-done.2 = bf16[4,512,3,64]{1,3,2,0:T(8,128)(2,1)} collective-permute-done((bf16[4,512,3,64]{1,3,2,0:T(8,128)(2,1)}, bf16[4,512,3,64]{1,3,2,0:T(8,128)(2,1)}, u32[]{:S(2)}, u32[]{:S(2)}) %collective-permute-start.2) | collective-permute-done | bytes 786464 | tf_op jit(solution)/shard_map/while/body/eval_jaxpr/ppermute | solution.py:20
  720.4 14.4 %collective-permute-done.3 = bf16[4,512,3,64]{1,3,2,0:T(8,128)(2,1)} collective-permute-done((bf16[4,512,3,64]{1,3,2,0:T(8,128)(2,1)}, bf16[4,512,3,64]{1,3,2,0:T(8,128)(2,1)}, u32[]{:S(2)}, u32[]{:S(2)}) %collective-permute-start.3) | collective-permute-done | bytes 786464 | tf_op jit(solution)/shard_map/while/body/eval_jaxpr/ppermute | solution.py:20
  737.2 14.4 %collective-permute-done = bf16[4,512,3,64]{1,3,2,0:T(8,128)(2,1)} collective-permute-done((bf16[4,512,3,64]{1,3,2,0:T(8,128)(2,1)}, bf16[4,512,3,64]{1,3,2,0:T(8,128)(2,1)}, u32[]{:S(2)}, u32[]{:S(2)}) %collective-permute-start) | collective-permute-done | bytes 786464 | tf_op jit(solution)/shard_map/while/body/eval_jaxpr/ppermute | solution.py:20
  751.6 16.9 %collective-permute-done.1 = bf16[4,512,3,64]{1,3,2,0:T(8,128)(2,1)} collective-permute-done((bf16[4,512,3,64]{1,3,2,0:T(8,128)(2,1)}, bf16[4,512,3,64]{1,3,2,0:T(8,128)(2,1)}, u32[]{:S(2)}, u32[]{:S(2)}) %collective-permute-start.1) | collective-permute-done | bytes 786464 | tf_op jit(solution)/shard_map/while/body/eval_jaxpr/ppermute | solution.py:20
  775.7 14.9 %conditional.6 = (f32[768,384]{0,1:T(8,128)}, f32[384]{0:T(512)}, f32[4,512,768]{2,1,0:T(8,128)}, bf16[4,512,384]{2,1,0:T(8,128)(2,1)}) conditional(s32[]{:T(128)} %convert_element_type.184, (bf16[4,512,192]{1,2,0:T(8,128)(2,1)S(1)}, s32[]{:T(128)}) %tuple.287, (bf16[4,512,768]{2,1,0:T(8,128)(2,1)}, bf16[4,512,192]{1,2,0:T(8,128)(2,1)S(1)}, ...), branch_computations={%region_27.28_spmd, %region_28.0_spmd} | conditional | flops 1208745728 | bytes 16617302 | solution.py:323
  838.2 23.3 %all-reduce.1 = (f32[192]{0:T(256)}, f32[768]{0:T(1024)}, f32[768]{0:T(1024)}, f32[768]{0:T(1024)}) all-reduce(f32[192]{0:T(256)} %reduce_sum.177, f32[768]{0:T(1024)} %convert_reduce_fusion.3, f32[768]{0:T(1024)} %get-tuple-element.1657, f32[768]{0:T(1024)} %convert_reduce_fusion.1), channel_id=1, replica_groups=mesh['seq'=2,'batch'=4,'tp'=4] {'seq','batch'}, use_global_device_ids=true, to_apply=%region_40.41 | all-reduce | flops 2496 | bytes 19968 | tf_op jit(solution)/shard_map/psum | solution.py:342
  865.7 46.1 %all-reduce = (f32[768]{0:T(1024)}, f32[768]{0:T(1024)}, f32[384]{0:T(512)}, f32[768]{0:T(1024)}, f32[768]{0:T(1024)}) all-reduce(f32[768]{0:T(1024)} %get-tuple-element.1531, f32[768]{0:T(1024)} %get-tuple-element.1536, f32[384]{0:T(512)} %get-tuple-element.1408, ...), channel_id=1, replica_groups=mesh['seq'=2,'batch'=4,'tp'=4] {'seq','batch','tp'}, use_global_device_ids=true, to_apply=%region_35.36 | all-reduce | flops 3456 | bytes 27648 | tf_op jit(solution)/shard_map/psum | solution.py:356
  914.4 12.4 %reduce-scatter.8.cloned.1.call-done = bf16[4,128,768]{2,1,0:T(8,128)(2,1)} async-done(((bf16[4,512,768]{2,1,0:T(8,128)(2,1)}), bf16[4,128,768]{2,1,0:T(8,128)(2,1)}) %reduce-scatter.8.cloned.1.call-update) | async-done | bytes 786448 | tf_op jit(solution)/shard_map/reduce_scatter | solution.py:206
  930.7 131.8 %all-reduce.6.cloned.1.call-done = f32[768,384]{1,0:T(8,128)} async-done(((f32[768,384]{1,0:T(8,128)}), f32[768,384]{1,0:T(8,128)}) %all-reduce.6.cloned.1.call-update) | async-done | bytes 1179664 | tf_op jit(solution)/shard_map/psum | solution.py:356
  1062.5 38.0 %reduce-scatter.14.cloned.1.call-done = bf16[4,128,384]{2,1,0:T(8,128)(2,1)} async-done(((bf16[4,512,384]{2,1,0:T(8,128)(2,1)}), bf16[4,128,384]{2,1,0:T(8,128)(2,1)}) %reduce-scatter.14.cloned.1.call-update) | async-done | bytes 393232 | tf_op jit(solution)/shard_map/reduce_scatter | solution.py:334
  1100.5 112.3 %all-reduce.8.cloned.1.call-done = (f32[768,192]{0,1:T(8,128)}, f32[768,192]{0,1:T(8,128)}, f32[192,768]{1,0:T(8,128)}, f32[768,768]{1,0:T(8,128)}, f32[768,768]{1,0:T(8,128)}) async-done(((f32[768,192]{0,1:T(8,128)}, f32[768,192]{0,1:T(8,128)}, f32[192,768]{1,0:T(8,128)}, f32[768,768]{1,0:T(8,128)}, f32[768,768]{1,0:T(8,128)}), (f32[768,192]{0,1:T(8,128)}, f32[768,192]{0,1:T(8,128)}, f32[192,768]{1,0:T(8,128)}, ...) | async-done | bytes 6488080 | tf_op jit(solution)/shard_map/psum | solution.py:342
  (315 shorter events, 278.6 us)
Async XLA Ops:
  7.2 400.6 %copy-start = (bf16[768,768]{1,0:T(8,128)(2,1)S(1)}, bf16[768,768]{1,0:T(8,128)(2,1)}, u32[]{:S(2)}) copy-start(bf16[768,768]{1,0:T(8,128)(2,1)} %param.54) | copy-start | bytes 3538948
  7.2 70.1 %all-gather.8.cloned.1.call-start = ((), (), s32[]{:S(2)}) async-start(), calls=%async_computation.5 | async-start | bytes 3932160 | tf_op jit(solution)/shard_map/all_gather | solution.py:136
  11.6 102.9 %all-gather.12.cloned.1.call-start = ((), (), s32[]{:S(2)}) async-start(), calls=%async_computation.7 | async-start | bytes 1966080 | tf_op jit(solution)/shard_map/all_gather | solution.py:138
  12.6 68.7 %copy-start.33 = (bf16[768,384]{1,0:T(8,128)(2,1)S(1)}, bf16[768,384]{1,0:T(8,128)(2,1)}, u32[]{:S(2)}) copy-start(bf16[768,384]{1,0:T(8,128)(2,1)} %param.46) | copy-start | bytes 1769476
  12.7 130.4 %all-gather.10.cloned.1.call-start = ((), (), s32[]{:S(2)}) async-start(), calls=%async_computation.6 | async-start | bytes 2359296 | tf_op jit(solution)/shard_map/all_gather | solution.py:188
  81.3 90.2 %all-gather.14.cloned.1.call-start = ((), (), s32[]{:S(2)}) async-start(), calls=%async_computation.8 | async-start | bytes 2359296 | tf_op jit(solution)/shard_map/all_gather | solution.py:189
  118.6 156.9 %reduce-scatter.6.cloned.1.call-start = ((), (), s32[]{:S(2)}) async-start(), calls=%async_computation.9 | async-start | bytes 3932160 | tf_op jit(solution)/shard_map/reduce_scatter | solution.py:197
  196.9 78.7 %copy-start.34 = (f32[768]{0:T(1024)S(1)}, f32[768]{0:T(1024)}, u32[]{:S(2)}) copy-start(f32[768]{0:T(1024)} %param.49) | copy-start | bytes 9220
  196.9 147.2 %all-gather.16.cloned.1.call-start = ((), (), s32[]{:S(2)}) async-start(), calls=%async_computation.10 | async-start | bytes 3932160 | tf_op jit(solution)/shard_map/all_gather | solution.py:202
  277.1 209.0 %copy-start.36 = (f32[4,128]{1,0:T(4,128)}, f32[4,128]{1,0:T(4,128)S(1)}, u32[]{:S(2)}) copy-start(f32[4,128]{1,0:T(4,128)S(1)} %broadcast_multiply_fusion.4) | copy-start | bytes 6148
  280.2 127.6 %all-gather.18.cloned.1.call-start = ((), (), s32[]{:S(2)}) async-start(), calls=%async_computation.12 | async-start | bytes 3932160 | tf_op jit(solution)/shard_map/all_gather | solution.py:137
  281.0 202.4 %reduce-scatter.10.cloned.1.call-start = ((), (), s32[]{:S(2)}) async-start(), calls=%async_computation.13 | async-start | bytes 3932160 | tf_op jit(solution)/shard_map/reduce_scatter | solution.py:215
  424.4 128.5 %all-gather.20.cloned.1.call-start = ((), (), s32[]{:S(2)}) async-start(), calls=%async_computation.14 | async-start | bytes 3932160 | tf_op jit(solution)/shard_map/all_gather | solution.py:223
  489.1 374.0 %reduce-scatter.12.cloned.1.call-start = ((), (), s32[]{:S(2)}) async-start(), calls=%async_computation.15 | async-start | bytes 3932160 | tf_op jit(solution)/shard_map/reduce_scatter | solution.py:331
  593.1 18.7 %collective-permute-start.2 = (bf16[4,512,3,64]{1,3,2,0:T(8,128)(2,1)}, bf16[4,512,3,64]{1,3,2,0:T(8,128)(2,1)}, u32[]{:S(2)}, u32[]{:S(2)}) collective-permute-start(bf16[4,512,3,64]{1,3,2,0:T(8,128)(2,1)} %convert_element_type.373), channel_id=1, source_target_pairs={{16,0},{0,16},{17,1},{1,17},{18,2},{2,18},{19,3},{3,19},{20,4},{4,... | collective-permute-start | bytes 2359304 | tf_op jit(solution)/shard_map/while/body/eval_jaxpr/ppermute | solution.py:20
  596.7 32.0 %collective-permute-start.3 = (bf16[4,512,3,64]{1,3,2,0:T(8,128)(2,1)}, bf16[4,512,3,64]{1,3,2,0:T(8,128)(2,1)}, u32[]{:S(2)}, u32[]{:S(2)}) collective-permute-start(bf16[4,512,3,64]{1,3,2,0:T(8,128)(2,1)} %convert_element_type.375), channel_id=1, source_target_pairs={{16,0},{0,16},{17,1},{1,17},{18,2},{2,18},{19,3},{3,19},{20,4},{4,... | collective-permute-start | bytes 2359304 | tf_op jit(solution)/shard_map/while/body/eval_jaxpr/ppermute | solution.py:20
  596.9 48.6 %collective-permute-start = (bf16[4,512,3,64]{1,3,2,0:T(8,128)(2,1)}, bf16[4,512,3,64]{1,3,2,0:T(8,128)(2,1)}, u32[]{:S(2)}, u32[]{:S(2)}) collective-permute-start(bf16[4,512,3,64]{1,3,2,0:T(8,128)(2,1)} %copy.125), channel_id=1, source_target_pairs={{16,0},{0,16},{17,1},{1,17},{18,2},{2,18},{19,3},{3,19},{20,4},{4,... | collective-permute-start | bytes 2359304 | tf_op jit(solution)/shard_map/while/body/eval_jaxpr/ppermute | solution.py:20
  598.1 64.2 %collective-permute-start.1 = (bf16[4,512,3,64]{1,3,2,0:T(8,128)(2,1)}, bf16[4,512,3,64]{1,3,2,0:T(8,128)(2,1)}, u32[]{:S(2)}, u32[]{:S(2)}) collective-permute-start(bf16[4,512,3,64]{1,3,2,0:T(8,128)(2,1)} %copy.126), channel_id=1, source_target_pairs={{16,0},{0,16},{17,1},{1,17},{18,2},{2,18},{19,3},{3,19},{20,4},{4,... | collective-permute-start | bytes 2359304 | tf_op jit(solution)/shard_map/while/body/eval_jaxpr/ppermute | solution.py:20
  673.0 44.9 %collective-permute-start.2 = (bf16[4,512,3,64]{1,3,2,0:T(8,128)(2,1)}, bf16[4,512,3,64]{1,3,2,0:T(8,128)(2,1)}, u32[]{:S(2)}, u32[]{:S(2)}) collective-permute-start(bf16[4,512,3,64]{1,3,2,0:T(8,128)(2,1)} %convert_element_type.373), channel_id=1, source_target_pairs={{16,0},{0,16},{17,1},{1,17},{18,2},{2,18},{19,3},{3,19},{20,4},{4,... | collective-permute-start | bytes 2359304 | tf_op jit(solution)/shard_map/while/body/eval_jaxpr/ppermute | solution.py:20
  703.7 31.1 %collective-permute-start.3 = (bf16[4,512,3,64]{1,3,2,0:T(8,128)(2,1)}, bf16[4,512,3,64]{1,3,2,0:T(8,128)(2,1)}, u32[]{:S(2)}, u32[]{:S(2)}) collective-permute-start(bf16[4,512,3,64]{1,3,2,0:T(8,128)(2,1)} %convert_element_type.375), channel_id=1, source_target_pairs={{16,0},{0,16},{17,1},{1,17},{18,2},{2,18},{19,3},{3,19},{20,4},{4,... | collective-permute-start | bytes 2359304 | tf_op jit(solution)/shard_map/while/body/eval_jaxpr/ppermute | solution.py:20
  703.7 47.9 %collective-permute-start = (bf16[4,512,3,64]{1,3,2,0:T(8,128)(2,1)}, bf16[4,512,3,64]{1,3,2,0:T(8,128)(2,1)}, u32[]{:S(2)}, u32[]{:S(2)}) collective-permute-start(bf16[4,512,3,64]{1,3,2,0:T(8,128)(2,1)} %copy.125), channel_id=1, source_target_pairs={{16,0},{0,16},{17,1},{1,17},{18,2},{2,18},{19,3},{3,19},{20,4},{4,... | collective-permute-start | bytes 2359304 | tf_op jit(solution)/shard_map/while/body/eval_jaxpr/ppermute | solution.py:20
  705.1 63.3 %collective-permute-start.1 = (bf16[4,512,3,64]{1,3,2,0:T(8,128)(2,1)}, bf16[4,512,3,64]{1,3,2,0:T(8,128)(2,1)}, u32[]{:S(2)}, u32[]{:S(2)}) collective-permute-start(bf16[4,512,3,64]{1,3,2,0:T(8,128)(2,1)} %copy.126), channel_id=1, source_target_pairs={{16,0},{0,16},{17,1},{1,17},{18,2},{2,18},{19,3},{3,19},{20,4},{4,... | collective-permute-start | bytes 2359304 | tf_op jit(solution)/shard_map/while/body/eval_jaxpr/ppermute | solution.py:20
  798.1 128.6 %reduce-scatter.8.cloned.1.call-start = ((), (), s32[]{:S(2)}) async-start(), calls=%async_computation.11 | async-start | bytes 3932160 | tf_op jit(solution)/shard_map/reduce_scatter | solution.py:206
  807.3 255.1 %all-reduce.6.cloned.1.call-start = ((), (), s32[]{:S(2)}) async-start(), calls=%async_computation.17 | async-start | bytes 2359296 | tf_op jit(solution)/shard_map/psum | solution.py:356
  810.1 290.4 %reduce-scatter.14.cloned.1.call-start = ((), (), s32[]{:S(2)}) async-start(), calls=%async_computation.16 | async-start | bytes 1966080 | tf_op jit(solution)/shard_map/reduce_scatter | solution.py:334
  810.8 401.9 %all-reduce.8.cloned.1.call-start = ((), (), s32[]{:S(2)}) async-start(), calls=%async_computation.18 | async-start | bytes 12976128 | tf_op jit(solution)/shard_map/psum | solution.py:342
  838.2 88.6 %copy-start.8 = (bf16[4,128,768]{2,1,0:T(8,128)(2,1)S(1)}, bf16[4,128,768]{2,1,0:T(8,128)(2,1)}, u32[]{:S(2)}) copy-start(bf16[4,128,768]{2,1,0:T(8,128)(2,1)} %reduce-scatter.6.cloned.1.call-done) | copy-start | bytes 2359300
  838.2 88.6 %copy-start.17 = (bf16[4,128,768]{2,1,0:T(8,128)(2,1)S(1)}, bf16[4,128,768]{2,1,0:T(8,128)(2,1)}, u32[]{:S(2)}) copy-start(bf16[4,128,768]{2,1,0:T(8,128)(2,1)} %param.40) | copy-start | bytes 2359300
  838.2 88.6 %copy-start.35 = (f32[768]{0:T(1024)S(1)}, f32[768]{0:T(1024)}, u32[]{:S(2)}) copy-start(f32[768]{0:T(1024)} %param.49) | copy-start | bytes 9220
  838.2 88.6 %copy-start.37 = (f32[4,128]{1,0:T(4,128)S(1)}, f32[4,128]{1,0:T(4,128)}, u32[]{:S(2)}) copy-start(f32[4,128]{1,0:T(4,128)} %copy-done.36) | copy-start | bytes 6148
  838.2 88.6 %copy-start.39 = (f32[768]{0:T(1024)S(1)}, f32[768]{0:T(1024)}, u32[]{:S(2)}) copy-start(f32[768]{0:T(1024)} %param.50) | copy-start | bytes 9220
  1062.5 154.2 %copy-start.24 = (f32[768,384]{1,0:T(8,128)S(1)}, f32[768,384]{1,0:T(8,128)}, u32[]{:S(2)}) copy-start(f32[768,384]{1,0:T(8,128)} %all-reduce.6.cloned.1.call-done) | copy-start | bytes 3538948
  (51 other events, 372.4 us)
Sparse Core Ops, SparseCore 0:
  11.7 65.5 all-gather.7
  79.5 35.0 all-gather.11
  116.1 26.8 all-gather.9
  144.4 27.0 all-gather.13
  197.0 78.4 reduce-scatter.5
  280.3 63.6 all-gather.15
  345.6 62.1 all-gather.17
  424.5 58.7 reduce-scatter.9
  489.3 63.6 all-gather.19
  798.2 64.8 reduce-scatter.11
  865.5 61.2 reduce-scatter.7
  932.0 130.4 all-reduce.5
  1065.5 34.9 reduce-scatter.13
  1106.5 106.2 all-reduce.7
where the time goes:
time: 1240 us; the launch traced here: 1230 us
  waiting for transfers between devices  862 us (70%)
  matrix products  127 us (10%)
  blocking collectives  69.4 us (6%)
  other arithmetic  66.8 us (5%)
  local copies, waits for them, and re-layouts  54.7 us (4%)
  starting transfers between devices  34.5 us (3%)
  between operations  14.7 us (1%)
    psum x1, waiting for transfers between devices, on_device(): lax.psum((grad_gain_one, grad_bias_one, grad_gain_two, grad_bias_two, gra...  132 us
    ppermute x8, waiting for transfers between devices, from_behind(): return lax.ppermute(block, axis, route)  117 us
    psum x1, waiting for transfers between devices, on_device(): lax.psum((grad_w_query, grad_w_key, grad_w_out, grad_w_up, grad_w_down, g...  112 us
    reduce_scatter x1, waiting for transfers between devices, on_device(): lax.psum_scatter(project(attended_low, w_out).astype(jnp.bfloat16), 'tp',...  78.6 us
    all_gather x1, waiting for transfers between devices, on_device(): lax.all_gather(normed_one.astype(jnp.bfloat16), 'tp', axis=1, tiled=True)  64.6 us
    all_gather x1, waiting for transfers between devices, on_device(): lax.all_gather(grad_middle.astype(jnp.bfloat16), 'tp', axis=1, tiled=True)  63.5 us
    all_gather x1, waiting for transfers between devices, on_device(): lax.all_gather(normed_two.astype(jnp.bfloat16), 'tp', axis=1, tiled=True)  62.5 us
    reduce_scatter x1, waiting for transfers between devices, on_device(): lax.psum_scatter(project_back(grad_hidden, w_up).astype(jnp.bfloat16), 't...  58.9 us
  transfers between devices with their start and end apart: 22, of which 22 were waited for; matrix products, arithmetic and copies ran while one was open for 8% of the time, Pallas kernels for 0%

commit v1 on v0

--- a/solution.py
+++ b/solution.py
@@ -3,6 +3,8 @@
 import jax
 import jax.numpy as jnp
 from jax import lax
+from jax.experimental import pallas as pl
+from jax.experimental.pallas import tpu as pltpu
 from jax.sharding import PartitionSpec as P
 
 HEADS = 12
@@ -379,6 +381,973 @@
     )
 
 
+BF = jnp.bfloat16
+F4 = jnp.float32
+MESH = pl.DeviceIdType.MESH
+QB = 256
+
+
+def dot(a, b):
+    return lax.dot_general(a, b, (((1,), (0,)), ((), ())), preferred_element_type=F4)
+
+
+def dot_nt(a, b):
+    return lax.dot_general(a, b, (((1,), (1,)), ((), ())), preferred_element_type=F4)
+
+
+def dot_tn(a, b):
+    return lax.dot_general(a, b, (((0,), (0,)), ((), ())), preferred_element_type=F4)
+
+
+def maybe(cond, act):
+    if cond is None:
+        act()
+    else:
+        pl.when(cond)(act)
+
+
+class Wire:
+    def __init__(self, copy, send_if=None, recv_if=None):
+        self.copy, self.send_if, self.recv_if = copy, send_if, recv_if
+
+    def start(self):
+        maybe(self.send_if, self.copy.start)
+
+    def arrived(self):
+        maybe(self.recv_if, self.copy.wait_recv)
+
+    def sent(self):
+        maybe(self.send_if, self.copy.wait_send)
+
+
+class Own:
+    def __init__(self, copy, when=None):
+        self.copy, self.when = copy, when
+
+    def start(self):
+        maybe(self.when, self.copy.start)
+
+    def arrived(self):
+        maybe(self.when, self.copy.wait)
+
+    def sent(self):
+        pass
+
+
+class Net:
+    def __init__(self, send_sems, recv_sems, own_sems):
+        self.send_sems, self.recv_sems, self.own_sems = send_sems, recv_sems, own_sems
+        self.n_send = self.n_recv = self.n_own = 0
+        self.all = []
+
+    def recv_slots(self, count):
+        self.n_recv += count
+        return self.n_recv - count
+
+    def wire(self, src, dst, device, send_if=None, recv_if=None, slot=None):
+        if slot is None:
+            slot = self.recv_slots(1)
+        copy = pltpu.make_async_remote_copy(
+            src_ref=src,
+            dst_ref=dst,
+            send_sem=self.send_sems.at[self.n_send],
+            recv_sem=self.recv_sems.at[slot],
+            device_id=device,
+            device_id_type=MESH,
+        )
+        self.n_send += 1
+        made = Wire(copy, send_if, recv_if)
+        self.all.append(made)
+        return made
+
+    def done(self, wire):
+        wire.sent()
+        self.all = [item for item in self.all if item is not wire]
+
+    def own(self, src, dst, when=None):
+        copy = pltpu.make_async_copy(src, dst, self.own_sems.at[self.n_own])
+        self.n_own += 1
+        return Own(copy, when)
+
+
+def norm_stats(values):
+    average = jnp.mean(values, axis=-1, keepdims=True)
+    centered = values - average
+    inverse = lax.rsqrt(jnp.mean(centered * centered, axis=-1, keepdims=True) + eps)
+    return centered * inverse, inverse
+
+
+def layer_kernel(
+    tokens, first, cot_in, seg, wa_in, wup_in, wdown_in, wval_in, bvec_in, vecs,
+    out, gtok, gfirst, f_up, f_down, f_wa, f_wv, f_small,
+    x_own, n1, segint, segrow, segcol, bvec, wa, wval, wup, wdown,
+    q, k, v, att, lse, mid, n2, cot,
+    mine, xs, xr, out_s, gm, gatt, gv_s,
+    gup, gdown, up_r1, up_r2, up_r3, down_r1, down_r2, down_r3,
+    gwa, wa_r1, wa_r2, wa_r3, gwv, wv_r1, wv_r2, wv_r3,
+    small, small_r, small_z, f_s, f_t, f_w, f_v,
+    send_sems, recv_sems, own_sems,
+):
+    s, b, t = lax.axis_index("seq"), lax.axis_index("batch"), lax.axis_index("tp")
+    y, c = lax.div(b, 2), lax.rem(b, 2)
+    sn, yn, cn = 1 - s, 1 - y, 1 - c
+    rows, blk, width = tokens.shape
+    half = rows * blk
+    length = 2 * half
+    net = Net(send_sems, recv_sems, own_sems)
+
+    def dev(ds, dy, dc, dt):
+        return (ds, 2 * dy + dc, dt)
+
+    def ring(step):
+        return lax.rem(t + step + rows, rows)
+
+    x_nbr, y_nbr, diag, mate = dev(sn, y, c, t), dev(s, yn, c, t), dev(sn, yn, c, t), dev(s, y, cn, t)
+    home = lax.div(t, 2) == c
+    away = lax.div(t, 2) != c
+    same, other = s == c, s != c
+
+    gate = pltpu.get_barrier_semaphore()
+    peers = [(s, 2 * yn + c, t), (sn, 2 * yn + c, t)]
+    for ds in range(2):
+        for dc in range(2):
+            for dt in range(rows):
+                if ds or dc or dt:
+                    peers.append((lax.rem(s + ds, 2), 2 * y + lax.rem(c + dc, 2), lax.rem(t + dt, rows)))
+    for peer in peers:
+        pl.semaphore_signal(gate, inc=1, device_id=peer, device_id_type=MESH)
+    pl.semaphore_wait(gate, len(peers))
+
+    def swap(src, dst):
+        wires = []
+        for step in range(rows):
+            r = ring(step)
+            if step == 0:
+                wires.append((
+                    net.wire(src.at[r], dst.at[t], dev(c, y, s, r), other, other),
+                    net.own(src.at[r], dst.at[t], same),
+                ))
+            else:
+                wires.append((net.wire(src.at[r], dst.at[t], dev(c, y, s, r)),))
+        return wires
+
+    def start_all(wires):
+        for group in wires:
+            for wire in group:
+                wire.start()
+
+    def arrived_all(wires):
+        for group in wires:
+            for wire in group:
+                wire.arrived()
+
+    seg_wire = net.wire(segint.at[0], segint.at[1], mate)
+    bvec_wires = []
+    for step in range(1, rows):
+        bvec_wires.append(net.wire(bvec.at[0], bvec.at[step], dev(s, y, c, ring(-step))))
+    wa_z = []
+    for step in range(1, rows):
+        wa_z.append(net.wire(
+            wa_in.at[:, s, y], wa.at[:, lax.rem(t, 2), s, y], dev(s, y, c, ring(step)),
+            home, lax.div(ring(-step), 2) == c,
+        ))
+    wa_own = net.own(wa_in, wa.at[:, lax.rem(t, 2)], home)
+    token_wires = swap(tokens, x_own)
+    wval_own = net.own(wval_in, wval, c == 0)
+    lanes_c = pl.ds(pl.multiple_of(c * (wup.shape[-1]), 128), wup.shape[-1])
+    up_own = net.own(wup_in.at[:, :, :, lanes_c], wup.at[0])
+    down_own = net.own(wdown_in.at[c], wdown.at[0])
+
+    bvec[0] = bvec_in[...]
+    row_ids = lax.broadcasted_iota(jnp.int32, seg.shape, 0)
+    seg_row = jnp.sum(jnp.where(row_ids == t, seg[...], 0), axis=0, keepdims=True)
+    segint[0] = jnp.broadcast_to(seg_row, segint.shape[1:])
+    for wire in wa_z:
+        wire.start()
+    seg_wire.start()
+    for wire in bvec_wires:
+        wire.start()
+    start_all(token_wires)
+    for own in (wa_own, wval_own, up_own, down_own):
+        own.start()
+
+    first_slot = net.recv_slots(2 * rows)
+    first_wires = []
+    for step in range(rows):
+        r = ring(step)
+        to = net.wire(
+            first.at[r], v.at[s * rows + t], dev(c, y, 1, r),
+            (c == 0) | (s == 0) if step == 0 else None, None, first_slot + s * rows + step,
+        )
+        first_wires.append(to)
+    first_own = net.own(first.at[t], v.at[s * rows + t], (c == 1) & (s == 1))
+
+    def first_arrived():
+        for source in range(2):
+            for step in range(rows):
+                def take(source=source, step=step):
+                    pltpu.make_async_remote_copy(
+                        src_ref=first.at[0], dst_ref=v.at[0], send_sem=send_sems.at[0],
+                        recv_sem=recv_sems.at[first_slot + source * rows + step],
+                        device_id=mate, device_id_type=MESH,
+                    ).wait_recv()
+                if source == 1 and step == 0:
+                    pl.when(s == 0)(take)
+                else:
+                    take()
+        first_own.arrived()
+
+    up_z, down_z = [], []
+    for step in range(1, rows):
+        up_z.append(net.wire(wup_in.at[s, y, :, lanes_c], wup.at[step, s, y], dev(s, y, c, ring(-step))))
+        down_z.append(net.wire(wdown_in.at[c, s, y], wdown.at[step, s, y], dev(s, y, c, ring(-step))))
+    rest = pl.ds(1, rows - 1)
+    up_one = net.wire(wup.at[rest, s, y], wup.at[rest, s, y], x_nbr)
+    up_two = net.wire(wup.at[rest, :, y], wup.at[rest, :, y], y_nbr)
+    down_one = net.wire(wdown.at[rest, s, y], wdown.at[rest, s, y], y_nbr)
+    down_two = net.wire(wdown.at[rest, s], wdown.at[rest, s], x_nbr)
+    cot_wires = swap(cot_in, cot.at[s])
+    cot_mate = net.wire(cot.at[c], cot.at[c], mate)
+
+    wa_plane = []
+    for step in range(1, rows):
+        ours = lax.div(ring(-step), 2) == c
+        piece = wa.at[:, lax.rem(ring(-step), 2), s, y]
+        wa_plane.append([net.wire(piece, piece, to, ours, ours) for to in (x_nbr, y_nbr, diag)])
+    for step in range(1, rows):
+        wa_z[step - 1].arrived()
+        for wire in wa_plane[step - 1]:
+            wire.start()
+
+    seg_wire.arrived()
+    chosen = jnp.where(same, segint[0], segint[1]).astype(F4)
+    segrow[...] = chosen
+    for part in range(length // 128):
+        piece = jnp.broadcast_to(chosen[0:1, part * 128:(part + 1) * 128], (128, 128))
+        segcol[part * 128:(part + 1) * 128, :] = piece.T
+
+    n1_wires = []
+    for step in range(rows):
+        place = ring(-step)
+        for wire in token_wires[step]:
+            wire.arrived()
+        unit, _ = norm_stats(x_own[place].astype(F4))
+        n1[c, place] = (unit * vecs[0:1, :] + vecs[1:2, :]).astype(BF)
+        wire = net.wire(n1.at[c, place], n1.at[c, place], mate)
+        wire.start()
+        n1_wires.append(wire)
+    for wire in first_wires:
+        wire.start()
+    first_own.start()
+    for wire in up_z + down_z:
+        wire.start()
+    for group in wa_plane:
+        for wire in group:
+            wire.arrived()
+    wa_own.arrived()
+    wval_own.arrived()
+    for wire in bvec_wires:
+        wire.arrived()
+    for wire in n1_wires:
+        wire.arrived()
+
+    heads_width = q.shape[1]
+    factor = HEAD_DIM ** (-0.5)
+    b_q = (bvec[lax.rem(2 * c + rows - t, rows), 1:2, :heads_width]
+           + bvec[lax.rem(2 * c + 1 + rows - t, rows), 1:2, :heads_width])
+    wq, wk, wo = (wa.at[i] for i in range(3))
+
+    def flat(ref_value):
+        return ref_value.reshape(-1, ref_value.shape[-1])
+
+    per_half = half // QB
+    per_blk = QB // blk
+
+    def n1_rows(i):
+        return flat(n1[lax.div(i, per_half), pl.ds(lax.rem(i, per_half) * per_blk, per_blk)])
+
+    def project_in(i, carry):
+        at = pl.ds(pl.multiple_of(i * QB, QB), QB)
+        block = n1_rows(i)
+        q[at, :] = ((dot_nt(block, flat(wq[...])) + b_q) * factor).astype(BF)
+        k_block = dot_nt(block, flat(wk[...]))
+        k[at, :] = k_block.astype(BF)
+        return carry
+
+    lax.fori_loop(0, length // QB, project_in, 0)
+
+    @pl.when(c == 0)
+    def _():
+        def fresh(i, carry):
+            got = (dot(n1_rows(i), wval[...]) + vecs[6:7, :heads_width]).astype(BF)
+            v[pl.ds(i * per_blk, per_blk)] = got.reshape(per_blk, blk, heads_width)
+            return carry
+
+        lax.fori_loop(0, length // QB, fresh, 0)
+
+    @pl.when(c == 1)
+    def _():
+        first_arrived()
+
+    pairs = heads_width // 128
+    n_q = length // QB
+    lane = lax.broadcasted_iota(jnp.int32, (1, 128), 1)
+    keeps = (lane < HEAD_DIM, lane >= HEAD_DIM)
+
+    def attend(j, bias, lsecol):
+        count = (j + 1) * QB
+        at = slice(j * QB, count)
+        key_pos = lax.broadcasted_iota(jnp.int32, (QB, count), 1)
+        query_pos = j * QB + lax.broadcasted_iota(jnp.int32, (QB, count), 0)
+        allowed = (segcol[at, 0:1] == segrow[0:1, :count]) & (key_pos <= query_pos)
+        bias[:, :count] = jnp.where(allowed, 0.0, far_below)
+        lsecol[...] = jnp.zeros_like(lsecol)
+
+        def pair(hp, carry):
+            lanes = pl.ds(pl.multiple_of(hp * 128, 128), 128)
+            q_pair = q[at, lanes]
+            k_pair = k[:count, lanes]
+            v_pair = flat(v[:count // blk, :, lanes])
+            total = None
+            for i in range(2):
+                scores = dot_nt(q_pair, jnp.where(keeps[i], k_pair, 0.0)) + bias[:, :count]
+                top = jnp.max(scores, axis=1, keepdims=True)
+                weights = jnp.exp(scores - top)
+                norm = jnp.sum(weights, axis=1, keepdims=True)
+                part = dot(weights.astype(BF), jnp.where(keeps[i], v_pair, 0.0)) * (1.0 / norm)
+                total = part if total is None else total + part
+                lsecol[...] = jnp.where(lane == 2 * hp + i, top + jnp.log(norm), lsecol[...])
+            att[at, lanes] = total.astype(BF)
+            return carry
+
+        lax.fori_loop(0, pairs, pair, 0)
+        lse[:, at] = lsecol[...].T[:lse.shape[0], :]
+
+    def relay_weights(stage):
+        if stage == 0:
+            for wire in up_z:
+                wire.arrived()
+            up_one.start()
+            for wire in down_z:
+                wire.arrived()
+            down_one.start()
+            start_all(cot_wires)
+        if stage == 1:
+            up_one.arrived()
+            up_two.start()
+            down_one.arrived()
+            down_two.start()
+
+    def attention(bias, lsecol):
+        for j in range(n_q):
+            if j == n_q - 1:
+                relay_weights(0)
+            attend(j, bias, lsecol)
+
+    pl.run_scoped(attention, pltpu.VMEM((QB, length), F4), pltpu.VMEM((QB, 128), F4))
+
+    att_wire = net.wire(xs.at[0], xr.at[0], mate)
+
+    def half_rows(h, i):
+        return pl.ds(pl.multiple_of(h * half + i * QB, QB), QB)
+
+    def out_proj(i, carry):
+        part = dot(att[half_rows(cn, i), :], flat(wo[...]))
+        xs[0, pl.ds(i * QB, QB), :] = part.astype(BF)
+        return carry
+
+    lax.fori_loop(0, per_half, out_proj, 0)
+    att_wire.start()
+
+    def out_proj_mine(i, carry):
+        mine[pl.ds(i * QB, QB), :] = dot(att[half_rows(c, i), :], flat(wo[...]))
+        return carry
+
+    lax.fori_loop(0, per_half, out_proj_mine, 0)
+    att_wire.arrived()
+
+    n2_wires = []
+    for i in range(rows):
+        at = slice(i * blk, (i + 1) * blk)
+        middle = x_own[i].astype(F4) + mine[at, :] + xr[0, at, :].astype(F4) + vecs[4:5, :]
+        mid[at, :] = middle
+        unit, _ = norm_stats(middle)
+        n2[c, i] = (unit * vecs[2:3, :] + vecs[3:4, :]).astype(BF)
+        wire = net.wire(n2.at[c, i], n2.at[c, i], mate)
+        wire.start()
+        n2_wires.append(wire)
+    relay_weights(1)
+    arrived_all(cot_wires)
+    cot_mate.start()
+    up_own.arrived()
+    down_own.arrived()
+    up_two.arrived()
+    down_two.arrived()
+
+    hid = wup.shape[-1]
+    back_wire = net.wire(xs.at[1], xr.at[1], mate)
+    mlp_wire = net.wire(xs.at[2], xr.at[2], mate)
+    out_wires = swap(out_s, out)
+    gm_wires = [net.wire(gm.at[c, i], gm.at[c, i], mate) for i in range(rows)]
+    up_rs = (net.wire(gup.at[:, sn], up_r1, x_nbr), net.wire(gup.at[:, s, yn], up_r2, y_nbr))
+    down_rs = (net.wire(gdown.at[:, :, yn], down_r1, y_nbr), net.wire(gdown.at[:, sn, y], down_r2, x_nbr))
+    up_rz = [net.wire(gup.at[i, s, y], up_r3.at[i], dev(s, y, c, ring(i))) for i in range(1, rows)]
+    down_rz = [net.wire(gdown.at[i, s, y], down_r3.at[i], dev(s, y, c, ring(i))) for i in range(1, rows)]
+    gelu_scale = math.sqrt(2.0 / math.pi)
+
+    def feed_forward(act, ghid, bup_sum, back_own):
+        bup_sum[...] = jnp.zeros_like(bup_sum)
+
+        def block(h, i, keep):
+            at = half_rows(h, i)
+            n2_block = flat(n2[h, pl.ds(i * per_blk, per_blk)])
+            cot_block = flat(cot[h, pl.ds(i * per_blk, per_blk)])
+            mlp = back = None
+            for p in range(rows):
+                cols = slice(p * hid, (p + 1) * hid)
+                w_u = flat(wup[p])
+                w_d = flat(wdown[p])
+                z = dot(n2_block, w_u) + bvec[p, 0:1, lanes_c]
+                z2 = z * z
+                th = jnp.tanh(gelu_scale * z * (1.0 + 0.044715 * z2))
+                cdf = 0.5 * (1.0 + th)
+                a = (z * cdf).astype(BF)
+                slope = cdf + 0.5 * z * (1.0 - th * th) * (gelu_scale * (1.0 + 3 * 0.044715 * z2))
+                act[at, cols] = a
+                part = dot(a, w_d)
+                mlp = part if mlp is None else mlp + part
+                g = (dot_nt(cot_block, w_d) * slope).astype(BF)
+                ghid[at, cols] = g
+                bup_sum[0:1, cols] += jnp.sum(g.astype(F4), axis=0, keepdims=True)
+                part = dot_nt(g, w_u)
+                back = part if back is None else back + part
+            to = pl.ds(pl.multiple_of(i * QB, QB), QB)
+            if keep:
+                mine[to, :] = mlp
+                back_own[to, :] = back
+            else:
+                xs[2, to, :] = mlp.astype(BF)
+                xs[1, to, :] = back.astype(BF)
+
+        def mine_block(i, carry):
+            block(c, i, True)
+            return carry
+
+        def mate_block(i, carry):
+            block(cn, i, False)
+            return carry
+
+        lax.fori_loop(0, per_half, mine_block, 0)
+        for wire in n2_wires:
+            wire.arrived()
+        cot_mate.arrived()
+        lax.fori_loop(0, per_half, mate_block, 0)
+        back_wire.start()
+        mlp_wire.start()
+
+        def down_grad(p, carry):
+            cols = pl.ds(pl.multiple_of(p * hid, 128), hid)
+            got = dot_tn(act[:, cols], flat(cot[...]))
+            gdown[p] = got.astype(BF).reshape(gdown.shape[1:])
+            return carry
+
+        lax.fori_loop(0, rows, down_grad, 0)
+        down_rs[0].start()
+
+        def up_grad(p, carry):
+            cols = pl.ds(pl.multiple_of(p * hid, 128), hid)
+            for m in range(2):
+                n2_part = flat(n2[:, :, :, m * (width // 2):(m + 1) * (width // 2)])
+                got = dot_tn(n2_part, ghid[:, cols])
+                gup[p, m] = got.astype(BF).reshape(gup.shape[2:])
+            return carry
+
+        lax.fori_loop(0, rows, up_grad, 0)
+        up_rs[0].start()
+        small[0] = jnp.zeros(small.shape[1:], F4)
+        for p in range(rows):
+            small[0, pl.ds(8 + ring(p), 1), lanes_c] = bup_sum[0:1, p * hid:(p + 1) * hid]
+
+        back_wire.arrived()
+        mlp_wire.arrived()
+        sums = [jnp.zeros((1, width), F4) for _ in range(4)]
+        for i in range(rows):
+            at = slice(i * blk, (i + 1) * blk)
+            middle = mid[at, :]
+            out_s[i] = (middle + mine[at, :] + xr[2, at, :].astype(F4) + vecs[5:6, :]).astype(BF)
+            unit, inverse = norm_stats(middle)
+            back = back_own[at, :] + xr[1, at, :].astype(F4)
+            cot_block = cot[c, i].astype(F4)
+            g_middle = cot_block + norm_back(back, unit, inverse, vecs[2:3, :])
+            mid[at, :] = g_middle
+            g_low = g_middle.astype(BF)
+            gm[c, i] = g_low
+            gm_wires[i].start()
+            for n, item in enumerate((back * unit, back, g_low.astype(F4), cot_block)):
+                sums[n] += jnp.sum(item, axis=0, keepdims=True)
+        for n in range(4):
+            small[0, 2 + n:3 + n, :] = sums[n]
+        start_all(out_wires)
+
+    pl.run_scoped(
+        feed_forward,
+        pltpu.VMEM((length, rows * hid), BF),
+        pltpu.VMEM((length, rows * hid), BF),
+        pltpu.VMEM((8, rows * hid), F4),
+        pltpu.VMEM((half, width), F4),
+    )
+
+    up_own_f = net.own(f_s.at[0], f_up.at[s, y, :, lanes_c])
+    up_ag = (
+        net.wire(f_s.at[0], f_up.at[s, y, :, lanes_c], x_nbr),
+        net.wire(f_up.at[:, y, :, lanes_c], f_up.at[:, y, :, lanes_c], y_nbr),
+        net.wire(f_up.at[:, :, :, lanes_c], f_up.at[:, :, :, lanes_c], mate),
+    )
+    down_own_f = net.own(f_t, f_down.at[c, s, y])
+    down_ag = (
+        net.wire(f_t, f_down.at[c, s, y], y_nbr),
+        net.wire(f_down.at[c, s], f_down.at[c, s], x_nbr),
+        net.wire(f_down.at[c], f_down.at[c], mate),
+    )
+
+    def add(one, two):
+        return (one.astype(F4) + two.astype(F4)).astype(BF)
+
+    def ffn_reduce(stage):
+        if stage == 0:
+            down_rs[0].arrived()
+            up_rs[0].arrived()
+
+            def one(p, carry):
+                gdown[p, :, y] = add(gdown[p, :, y], down_r1[p])
+                gup[p, s] = add(gup[p, s], up_r1[p])
+                return carry
+
+            lax.fori_loop(0, rows, one, 0)
+            down_rs[1].start()
+            up_rs[1].start()
+        if stage == 1:
+            down_rs[1].arrived()
+            up_rs[1].arrived()
+
+            def two(p, carry):
+                gdown[p, s, y] = add(gdown[p, s, y], down_r2[p])
+                gup[p, s, y] = add(gup[p, s, y], up_r2[p])
+                return carry
+
+            lax.fori_loop(0, rows, two, 0)
+            for wire in down_rz + up_rz:
+                wire.start()
+        if stage == 2:
+            for wire in down_rz + up_rz:
+                wire.arrived()
+            for to, kept, got in ((f_s.at[0], gup[0, s, y], up_r3), (f_t, gdown[0, s, y], down_r3)):
+                total = kept.astype(F4)
+                for i in range(1, rows):
+                    total += got[i].astype(F4)
+                to[...] = total.astype(BF)
+            for wire in (up_own_f, down_own_f, up_ag[0], down_ag[0]):
+                wire.start()
+        if stage == 3:
+            for wire in (up_own_f, down_own_f, up_ag[0], down_ag[0]):
+                wire.arrived()
+            up_ag[1].start()
+            down_ag[1].start()
+        if stage == 4:
+            up_ag[1].arrived()
+            down_ag[1].arrived()
+            up_ag[2].start()
+            down_ag[2].start()
+        if stage == 5:
+            up_ag[2].arrived()
+            down_ag[2].arrived()
+
+    back1_wire = net.wire(xs.at[0], xr.at[0], mate)
+    gtok_wires = swap(out_s, gtok)
+    gfirst_slot = net.recv_slots(rows)
+    gfirst_wires = []
+    for h in range(2):
+        for step in range(rows):
+            j = ring(step)
+            to_me = (c == 1) & (s == h) & (s == 1) if step == 0 else None
+            fine = (c == 1) & jnp.logical_not(to_me) if step == 0 else c == 1
+            gfirst_wires.append(net.wire(
+                gv_s.at[h * rows + j], gfirst.at[t], dev(h, y, s, j), fine, None, gfirst_slot + step,
+            ))
+    gfirst_own = net.own(gv_s.at[rows + t], gfirst.at[t], (c == 1) & (s == 1))
+    wa_rs = (net.wire(gwa.at[:, :, sn], wa_r1, x_nbr), net.wire(gwa.at[:, :, s, yn], wa_r2, y_nbr))
+    wa_rz = []
+    for step in range(1, rows):
+        to = ring(step)
+        wa_rz.append(net.wire(
+            gwa.at[:, lax.rem(to, 2), s, y], wa_r3.at[step], dev(s, y, c, to), lax.div(to, 2) == c, home,
+        ))
+    wa_own_f = net.own(f_w, f_wa.at[:, s, y], home)
+    wa_ag = (
+        net.wire(f_w, f_wa.at[:, s, y], x_nbr, home, home),
+        net.wire(f_wa.at[:, :, y], f_wa.at[:, :, y], y_nbr, home, home),
+        net.wire(f_wa, f_wa, mate, home, away),
+    )
+    lead, follow = c == 0, c == 1
+    wv_rs = (
+        net.wire(gwv.at[sn], wv_r1, x_nbr, lead, lead),
+        net.wire(gwv.at[s, yn], wv_r2, y_nbr, lead, lead),
+    )
+    wv_rz = [
+        net.wire(wv_r3.at[t], wv_r3.at[t], dev(s, y, c, ring(step)), lead, lead) for step in range(1, rows)
+    ]
+    wv_own_f = net.own(f_v, f_wv.at[s, y], lead)
+    wv_ag = (
+        net.wire(f_v, f_wv.at[s, y], x_nbr, lead, lead),
+        net.wire(f_wv.at[:, y], f_wv.at[:, y], y_nbr, lead, lead),
+        net.wire(f_wv, f_wv, mate, lead, follow),
+    )
+    small_ar = [net.wire(small.at[i], small_r.at[i], to) for i, to in enumerate((mate, x_nbr, y_nbr))]
+    small_rz = [net.wire(small_z.at[t], small_z.at[t], dev(s, y, c, ring(step))) for step in range(1, rows)]
+
+    def small_reduce(stage):
+        if stage == 0:
+            small_ar[0].start()
+        elif stage < 3:
+            small_ar[stage - 1].arrived()
+            small[stage] = small[stage - 1] + small_r[stage - 1]
+            small_ar[stage].start()
+        elif stage == 3:
+            small_ar[2].arrived()
+            small_z[t] = small[2] + small_r[2]
+            for wire in small_rz:
+                wire.start()
+        else:
+            for wire in small_rz:
+                wire.arrived()
+            f_small[...] = (small_z[0] + small_z[1]) + (small_z[2] + small_z[3])
+
+    heads_here = heads_width // HEAD_DIM
+    pick_head = lax.broadcasted_iota(jnp.int32, (lse.shape[0], heads_width), 1) // HEAD_DIM
+    pick = (pick_head == lax.broadcasted_iota(jnp.int32, pick_head.shape, 0)).astype(BF)
+
+    def attention_back(gk, gv, delta, tmp, gq, kt, gqt, bias_t):
+        kt[...] = k[...].T
+        gk[...] = jnp.zeros_like(gk)
+        gv[...] = jnp.zeros_like(gv)
+
+        def grad_att(h, i):
+            at = half_rows(h, i)
+            block = flat(gm[h, pl.ds(i * per_blk, per_blk)])
+            low = dot_nt(block, flat(wo[...])).astype(BF)
+            gatt[at, :] = low
+            product = low.astype(F4) * att[at, :].astype(F4)
+            high = product.astype(BF)
+            rest_of = (product - high.astype(F4)).astype(BF)
+            delta[:, at] = dot_nt(pick, high) + dot_nt(pick, rest_of)
+
+        def grad_att_mine(i, carry):
+            grad_att(c, i)
+            return carry
+
+        def grad_att_mate(i, carry):
+            grad_att(cn, i)
+            return carry
+
+        lax.fori_loop(0, per_half, grad_att_mine, 0)
+        for wire in gm_wires:
+            wire.arrived()
+        lax.fori_loop(0, per_half, grad_att_mate, 0)
+        gwa[2] = dot_tn(att[...], flat(gm[...])).astype(BF).reshape(gwa.shape[1:])
+
+        def back_block(j):
+            count = (j + 1) * QB
+            at = slice(j * QB, count)
+            key_pos = lax.broadcasted_iota(jnp.int32, (count, QB), 0)
+            query_pos = j * QB + lax.broadcasted_iota(jnp.int32, (count, QB), 1)
+            allowed = (segcol[:count, 0:1] == segrow[0:1, at]) & (key_pos <= query_pos)
+            bias_t[:count, :] = jnp.where(allowed, 0.0, far_below)
+
+            def pair(hp, carry):
+                lanes = pl.ds(pl.multiple_of(hp * 128, 128), 128)
+                q_pair = q[at, lanes]
+                k_pair = k[:count, lanes]
+                v_pair = flat(v[:count // blk, :, lanes])
+                ga_pair = gatt[at, lanes]
+                sum_k = sum_v = None
+                for i in range(2):
+                    head = 2 * hp + i
+                    scores = dot_nt(jnp.where(keeps[i], k_pair, 0.0), q_pair) + bias_t[:count, :]
+                    probs = jnp.exp(scores - lse[pl.ds(head, 1), at])
+                    grad_prob = dot_nt(jnp.where(keeps[i], v_pair, 0.0), ga_pair)
+                    grad_score = (probs * (grad_prob - delta[pl.ds(head, 1), at])).astype(BF)
+                    part_v = dot(probs.astype(BF), jnp.where(keeps[i], ga_pair, 0.0))
+                    part_k = dot(grad_score, jnp.where(keeps[i], q_pair, 0.0))
+                    sum_v = part_v if sum_v is None else sum_v + part_v
+                    sum_k = part_k if sum_k is None else sum_k + part_k
+                    channels = pl.ds(pl.multiple_of(hp * 128 + i * HEAD_DIM, HEAD_DIM), HEAD_DIM)
+                    gqt[channels, at] = (dot(kt[channels, :count], grad_score) * factor).astype(BF)
+                gk[:count, lanes] += sum_k
+                gv[:count, lanes] += sum_v
+                return carry
+
+            lax.fori_loop(0, pairs, pair, 0)
+
+        for j in range(n_q):
+            back_block(j)
+            if j >= 1:
+                ffn_reduce(j - 1)
+
+        gq[...] = gqt[...].T
+        gk_low = gk[...].astype(BF)
+        k[...] = gk_low
+        gv_s[...] = gv[...].astype(BF).reshape(gv_s.shape)
+
+        def back_rows(h, i):
+            at = half_rows(h, i)
+            tmp[...] = dot(gq[at, :], flat(wq[...])) + dot(k[at, :], flat(wk[...]))
+
+            @pl.when(lead)
+            def _():
+                block = flat(gv_s[pl.ds(h * rows + i * per_blk, per_blk)])
+                tmp[...] += dot_nt(block, wval[...])
+
+        def back_mate(i, carry):
+            back_rows(cn, i)
+            xs[0, pl.ds(pl.multiple_of(i * QB, QB), QB), :] = tmp[...].astype(BF)
+            return carry
+
+        def back_mine(i, carry):
+            back_rows(c, i)
+            mine[pl.ds(pl.multiple_of(i * QB, QB), QB), :] = tmp[...]
+            return carry
+
+        net.done(att_wire)
+        lax.fori_loop(0, per_half, back_mate, 0)
+        back1_wire.start()
+        for wire in gfirst_wires:
+            wire.start()
+        gfirst_own.start()
+        lax.fori_loop(0, per_half, back_mine, 0)
+        n1_all = flat(n1[...])
+        gwa[0] = dot(gqt[...], n1_all).astype(BF).reshape(gwa.shape[1:])
+        gwa[1] = dot_tn(k[...], n1_all).astype(BF).reshape(gwa.shape[1:])
+        wa_rs[0].start()
+        small[0, 7:8, lanes_h] = jnp.sum(gq[...].astype(F4), axis=0, keepdims=True)
+
+        @pl.when(lead)
+        def _():
+            gv_low = flat(gv_s[...])
+            gwv[...] = dot_tn(gv_low, n1_all).astype(BF).reshape(gwv.shape)
+            small[0, 6:7, :heads_width] = jnp.sum(gv_low.astype(F4), axis=0, keepdims=True)
+
+        wv_rs[0].start()
+
+    lanes_h = pl.ds(pl.multiple_of(c * heads_width, 128), heads_width)
+    pl.run_scoped(
+        attention_back,
+        pltpu.VMEM((length, heads_width), F4),
+        pltpu.VMEM((length, heads_width), F4),
+        pltpu.VMEM((lse.shape[0], length), F4),
+        pltpu.VMEM((QB, width), F4),
+        pltpu.VMEM((length, heads_width), BF),
+        pltpu.VMEM((heads_width, length), BF),
+        pltpu.VMEM((heads_width, length), BF),
+        pltpu.VMEM((length, QB), F4),
+    )
+
+    back1_wire.arrived()
+    for group in out_wires:
+        net.done(group[0])
+    out_wires[0][1].arrived()
+    gain_sum = jnp.zeros((1, width), F4)
+    bias_sum = jnp.zeros((1, width), F4)
+    for i in range(rows):
+        at = slice(i * blk, (i + 1) * blk)
+        unit, inverse = norm_stats(x_own[i].astype(F4))
+        back = mine[at, :] + xr[0, at, :].astype(F4)
+        gain_sum += jnp.sum(back * unit, axis=0, keepdims=True)
+        bias_sum += jnp.sum(back, axis=0, keepdims=True)
+        out_s[i] = (mid[at, :] + norm_back(back, unit, inverse, vecs[0:1, :])).astype(BF)
+    small[0, 0:1, :] = gain_sum
+    small[0, 1:2, :] = bias_sum
+    start_all(gtok_wires)
+    small_reduce(0)
+
+    wa_rs[0].arrived()
+    gwa[:, :, s] = add(gwa[:, :, s], wa_r1[...])
+    wa_rs[1].start()
+
+    @pl.when(lead)
+    def _():
+        wv_rs[0].copy.wait_recv()
+        gwv[s] = add(gwv[s], wv_r1[...])
+        wv_rs[1].copy.start()
+
+    small_reduce(1)
+    ffn_reduce(3)
+    small_reduce(2)
+    wa_rs[1].arrived()
+    gwa[:, :, s, y] = add(gwa[:, :, s, y], wa_r2[...])
+    for wire in wa_rz:
+        wire.start()
+
+    @pl.when(lead)
+    def _():
+        wv_rs[1].copy.wait_recv()
+        wv_r3[t] = add(gwv[s, y], wv_r2[...])
+        for wire in wv_rz:
+            wire.copy.start()
+
+    small_reduce(3)
+    ffn_reduce(4)
+
+    @pl.when(home)
+    def _():
+        for wire in wa_rz:
+            wire.copy.wait_recv()
+        total = gwa[:, lax.rem(t, 2), s, y].astype(F4)
+        for i in range(1, rows):
+            total += wa_r3[i].astype(F4)
+        f_w[...] = total.astype(BF)
+
+    wa_own_f.start()
+    wa_ag[0].start()
+
+    @pl.when(lead)
+    def _():
+        for wire in wv_rz:
+            wire.copy.wait_recv()
+        parts = [wv_r3[i].astype(F4) for i in range(rows)]
+        f_v[...] = ((parts[0] + parts[1]) + (parts[2] + parts[3])).astype(BF)
+
+    wv_own_f.start()
+    wv_ag[0].start()
+    small_reduce(4)
+    for stage in range(2):
+        for wire in ((wa_own_f, wv_own_f) if stage == 0 else ()) + (wa_ag[stage], wv_ag[stage]):
+            wire.arrived()
+        wa_ag[stage + 1].start()
+        wv_ag[stage + 1].start()
+    ffn_reduce(5)
+    wa_ag[2].arrived()
+    wv_ag[2].arrived()
+    for group in out_wires:
+        group[0].arrived()
+    arrived_all(gtok_wires)
+    for step in range(rows):
+        def take(step=step):
+            pltpu.make_async_remote_copy(
+                src_ref=gv_s.at[0], dst_ref=gfirst.at[0], send_sem=send_sems.at[0],
+                recv_sem=recv_sems.at[gfirst_slot + step], device_id=mate, device_id_type=MESH,
+            ).wait_recv()
+        if step == 0:
+            pl.when((c == 0) | (s == 0))(take)
+        else:
+            take()
+    gfirst_own.arrived()
+    for wire in net.all:
+        wire.sent()
+
+
+def whole_layer(
+    tokens, first_values, segment_ids, cotangent, norm1_gain, norm1_bias, w_query, b_query, w_key,
+    w_value, b_value, w_out, b_out, norm2_gain, norm2_bias, w_up, b_up, w_down, b_down,
+):
+    rows, blk, width = tokens.shape
+    half = rows * blk
+    length = 2 * half
+    valf = w_value.shape[1]
+    tp_width = w_query.shape[1]
+    hid = w_up.shape[1] // 2
+    t = lax.axis_index("tp")
+    wa_in = jnp.stack([w_query.T, w_key.T, w_out]).reshape(3, 2, 2, tp_width // 4, width)
+    odd = lax.rem(t, 2) == 1
+    b_q = jnp.where(odd, jnp.pad(b_query, (tp_width, width - 2 * tp_width)), jnp.pad(b_query, (0, width - tp_width)))
+    bvec = jnp.concatenate([b_up[None], b_q[None], jnp.zeros((6, width), F4)])
+    vecs = jnp.stack([
+        norm1_gain, norm1_bias, norm2_gain, norm2_bias, b_out, b_down,
+        jnp.pad(b_value, (0, width - valf)), jnp.zeros((width,), F4),
+    ])
+    hbm = pl.BlockSpec(memory_space=pl.ANY)
+    vmem = pl.BlockSpec(memory_space=pltpu.VMEM)
+    piece = tp_width // 4
+    up_rows, down_rows = width // 4, hid // 4
+
+    def of(*shape, dtype=BF):
+        return jax.ShapeDtypeStruct(shape, dtype)
+
+    def room(*shape, dtype=BF):
+        return pltpu.VMEM(shape, dtype)
+
+    outs = (
+        of(rows, blk, width), of(rows, blk, width), of(rows, blk, valf),
+        of(2, 2, up_rows, 2 * hid), of(2, 2, 2, down_rows, width),
+        of(3, 2, 2, piece, width), of(2, 2, valf // 4, width), of(16, width, dtype=F4),
+    )
+    scratch = [
+        room(rows, blk, width), room(2, rows, blk, width), room(2, 8, length, dtype=jnp.int32),
+        room(8, length, dtype=F4), room(length, 128, dtype=F4), room(rows, 8, width, dtype=F4),
+        room(3, 2, 2, 2, piece, width), room(width, valf),
+        room(rows, 2, 2, up_rows, hid), room(rows, 2, 2, down_rows, width),
+        room(length, 2 * tp_width), room(length, 2 * tp_width), room(2 * rows, blk, valf),
+        room(length, 2 * tp_width), room(16, length, dtype=F4),
+        room(half, width, dtype=F4), room(2, rows, blk, width), room(2, rows, blk, width),
+        room(half, width, dtype=F4), room(3, half, width), room(3, half, width),
+        room(rows, blk, width), room(2, rows, blk, width),
+        room(length, 2 * tp_width), room(2 * rows, blk, valf),
+        room(rows, 2, 2, up_rows, hid), room(rows, 2, 2, down_rows, width),
+        room(rows, 2, up_rows, hid), room(rows, up_rows, hid), room(rows, up_rows, hid),
+        room(rows, 2, down_rows, width), room(rows, down_rows, width), room(rows, down_rows, width),
+        room(3, 2, 2, 2, piece, width), room(3, 2, 2, piece, width), room(3, 2, piece, width), room(rows, 3, piece, width),
+        room(2, 2, valf // 4, width), room(2, valf // 4, width), room(valf // 4, width), room(rows, valf // 4, width),
+        room(3, 16, width, dtype=F4), room(3, 16, width, dtype=F4), room(rows, 16, width, dtype=F4),
+        room(1, up_rows, hid), room(down_rows, width), room(3, piece, width), room(valf // 4, width),
+        pltpu.SemaphoreType.DMA((SENDS,)), pltpu.SemaphoreType.DMA((RECVS,)), pltpu.SemaphoreType.DMA((OWNS,)),
+    ]
+    out, gtok, gfirst, f_up, f_down, f_wa, f_wv, f_small = pl.pallas_call(
+        layer_kernel,
+        out_shape=outs,
+        in_specs=[hbm, hbm, hbm, vmem, hbm, hbm, hbm, hbm, vmem, vmem],
+        out_specs=(hbm,) * 7 + (vmem,),
+        scratch_shapes=scratch,
+        compiler_params=pltpu.CompilerParams(
+            collective_id=0, has_side_effects=True, vmem_limit_bytes=VMEM_BYTES
+        ),
+    )(
+        tokens, first_values, cotangent, segment_ids, wa_in,
+        w_up.reshape(2, 2, up_rows, 2 * hid), w_down.reshape(2, 2, 2, down_rows, width), w_value, bvec, vecs,
+    )
+    wa_flat = f_wa.reshape(3, tp_width, width).astype(F4)
+    grad_b_query = lax.dynamic_slice(f_small, (7, t * tp_width), (1, tp_width))[0]
+    grad_b_up = lax.dynamic_slice(f_small, (8 + t, 0), (1, width))[0]
+    return (
+        out,
+        gtok.astype(F4),
+        gfirst,
+        f_small[0],
+        f_small[1],
+        wa_flat[0].T,
+        grad_b_query,
+        wa_flat[1].T,
+        f_wv.reshape(valf, width).astype(F4).T,
+        f_small[6, :valf],
+        wa_flat[2],
+        f_small[4],
+        f_small[2],
+        f_small[3],
+        f_up.reshape(width, 2 * hid).astype(F4),
+        grad_b_up,
+        f_down.reshape(2 * hid, width).astype(F4),
+        f_small[5],
+    )
+
+
+SENDS = 120
+RECVS = 120
+OWNS = 16
+VMEM_BYTES = 63 * 1024 * 1024
+
+
+def fits(mesh):
+    return mesh.shape["seq"] == 2 and mesh.shape["batch"] == 4 and mesh.shape["tp"] == 4
+
+
 def solution(mesh):
     placed = (
         P("batch", ("seq", "tp"), None),
@@ -402,7 +1371,7 @@
         P(),
     )
     return jax.shard_map(
-        on_device,
+        whole_layer if fits(mesh) else on_device,
         mesh=mesh,
         in_specs=placed,
         out_specs=(

time: 1240 us -> 311 us (0.25)
  waiting for transfers between devices: 862 us -> 0 us
  Pallas kernels: 0 us -> 289 us
  matrix products: 127 us -> 0 us
  blocking collectives: 69.4 us -> 0 us
  other arithmetic: 66.8 us -> 8.35 us
  local copies, waits for them, and re-layouts: 54.7 us -> 11.4 us
  starting transfers between devices: 34.5 us -> 0 us
  between operations: 14.7 us -> 0.86 us
    all_gather x7 -> x0, waiting for transfers between devices: 309 us -> none  [the longest x1 64.6 us: on_device(): lax.all_gather(normed_one.astype(jnp.bfloat16), 'tp', axis=1, tiled=True)]
    pallas_call x0 -> x1, Pallas kernels: none -> 289 us  [whole_layer(): pl.pallas_call(layer_kernel, out_shape=outs, in_specs=[hbm, hbm, hbm, vme...]
    psum x2 -> x0, waiting for transfers between devices: 244 us -> none  [the longest x1 132 us: on_device(): lax.psum((grad_gain_one, grad_bias_one, grad_gain_two, grad_bias_two, gra...]
    reduce_scatter x5 -> x0, waiting for transfers between devices: 190 us -> none  [the longest x1 78.6 us: on_device(): lax.psum_scatter(project(attended_low, w_out).astype(jnp.bfloat16), 'tp',...]
    dot_general x32 -> x0, matrix products: 127 us -> none  [the longest x6 33.8 us: project_back(): jnp.einsum('rte,de->rtd', grads, weight, preferred_element_type=jnp.float32)]
    ppermute x8 -> x0, waiting for transfers between devices: 117 us -> none  [from_behind(): return lax.ppermute(block, axis, route)]
    psum x2 -> x0, blocking collectives: 69.4 us -> none  [the longest x1 46.1 us: on_device(): lax.psum((grad_gain_one, grad_bias_one, grad_gain_two, grad_bias_two, gra...]
    ppermute x8 -> x0, starting transfers between devices: 32.7 us -> none  [from_behind(): return lax.ppermute(block, axis, route)]
  transfers between devices with their start and end apart: 22 -> 0, of which waited for: 22 -> 0; matrix products, arithmetic and copies ran while one was open for 8% -> 0% of each run, Pallas kernels for 0% -> 0%
where the time goes in v1:
time: 311 us; the launch traced here: 310 us
  Pallas kernels  289 us (93%)
  local copies, waits for them, and re-layouts  11.4 us (4%)
  other arithmetic  8.35 us (3%)
    pallas_call x1, Pallas kernels, whole_layer(): pl.pallas_call(layer_kernel, out_shape=outs, in_specs=[hbm, hbm, hbm, vme...  289 us

profile of v1, /device:TPU:1, one launch (start us, length us, event | category | flops | bytes accessed | tf_op | source)
XLA Modules:
  0.0 309.9 jit_solution(698482918319626716)
XLA Ops:
  0.7 0.0 copy-start.12
  0.7 0.0 copy-start.6
  0.7 0.0 copy-start.7
  0.7 0.0 copy-start.8
  0.7 0.0 copy-start.9
  0.7 0.0 copy-start.10
  0.7 0.0 copy-start.11
  0.7 0.8 pad_select_fusion
  1.6 0.7 broadcast_in_dim.9
  2.3 0.1 pad.17.clone
  2.3 0.7 maximum_maximum_fusion.bvec_in
  3.0 2.1 pad_maximum_fusion.wa_in
  5.2 0.0 copy-done.12
  5.2 0.0 copy-done.6
  5.2 0.0 copy-done.7
  5.2 0.0 copy-done.9
  5.3 0.7 stack.47.vecs
  6.0 289.3 %shard_map.322 = (bf16[4,128,768]{2,1,0:T(8,128)(2,1)}, bf16[4,128,768]{2,1,0:T(8,128)(2,1)}, bf16[4,128,384]{2,1,0:T(8,128)(2,1)}, bf16[2,2,192,768]{3,2,1,0:T(...) custom-call(bf16[4,128,768]{2,1,0:T(8,128)(2,1)} %tokens.1, ...), custom_call_target="tpu_custom_call" | custom-call | tf_op jit(solution)/shard_map/pallas_call | solution.py:1303
  295.3 1.6 slice_reduce_fusion
  296.9 1.3 constant_dynamic-slice_fusion
  298.3 2.4 fusion
  300.7 1.3 slice_reduce_fusion.6
  302.0 0.1 bitcast_convert_fusion.2
  302.2 1.4 copy.37
  303.6 1.7 bitcast_convert_fusion
  305.2 1.7 bitcast_convert_fusion.1
  306.9 0.0 copy-done.3
  306.9 1.3 convert_element_type.29
  308.1 0.1 copy-done.2
  308.2 0.9 copy.40
  309.1 0.0 copy-done.5
  309.2 0.7 copy.41
  (23 shorter events, 0.1 us)
Async XLA Ops:
  0.7 4.5 %copy-start.12 = (f32[384]{0:T(512)S(1)}, f32[384]{0:T(512)}, u32[]{:S(2)}) copy-start(f32[384]{0:T(512)} %param.29) | copy-start | bytes 4612
  0.7 4.5 %copy-start.6 = (f32[768]{0:T(1024)S(1)}, f32[768]{0:T(1024)}, u32[]{:S(2)}) copy-start(f32[768]{0:T(1024)} %param.23) | copy-start | bytes 9220
  0.7 4.5 %copy-start.7 = (f32[768]{0:T(1024)S(1)}, f32[768]{0:T(1024)}, u32[]{:S(2)}) copy-start(f32[768]{0:T(1024)} %param.24) | copy-start | bytes 9220
  0.7 4.5 %copy-start.8 = (f32[768]{0:T(1024)S(1)}, f32[768]{0:T(1024)}, u32[]{:S(2)}) copy-start(f32[768]{0:T(1024)} %param.32) | copy-start | bytes 9220
  0.7 4.6 %copy-start.9 = (f32[768]{0:T(1024)S(1)}, f32[768]{0:T(1024)}, u32[]{:S(2)}) copy-start(f32[768]{0:T(1024)} %param.33) | copy-start | bytes 9220
  0.7 4.6 %copy-start.10 = (f32[768]{0:T(1024)S(1)}, f32[768]{0:T(1024)}, u32[]{:S(2)}) copy-start(f32[768]{0:T(1024)} %param.31) | copy-start | bytes 9220
  0.7 4.6 %copy-start.11 = (f32[768]{0:T(1024)S(1)}, f32[768]{0:T(1024)}, u32[]{:S(2)}) copy-start(f32[768]{0:T(1024)} %param.37) | copy-start | bytes 9220
  298.3 3.8 %copy-start.4 = (bf16[2,2,96,768]{3,2,1,0:T(8,128)(2,1)S(1)}, bf16[2,2,96,768]{3,2,1,0:T(8,128)(2,1)}, u32[]{:S(2)}) copy-start(bf16[2,2,96,768]{3,2,1,0:T(8,128)(2,1)} %get-tuple-element.31) | copy-start | bytes 1769476
  302.2 1.4 copy-start.1
  303.5 1.7 copy-start
  305.2 1.7 copy-start.3
  306.9 1.4 copy-start.2
  308.1 1.0 copy-start.5

commit v2 on v1

--- a/solution.py
+++ b/solution.py
@@ -484,8 +484,8 @@
     q, k, v, att, lse, mid, n2, cot,
     mine, xs, xr, out_s, gm, gatt, gv_s,
     gup, gdown, up_r1, up_r2, up_r3, down_r1, down_r2, down_r3,
-    gwa, wa_r1, wa_r2, wa_r3, gwv, wv_r1, wv_r2, wv_r3,
-    small, small_r, small_z, f_s, f_t, f_w, f_v,
+    gwa, wa_r1, wa_r2, wa_r3, gwv, wv_r1, wv_r3,
+    small, small_p, small_z, f_s, f_t, f_w, f_v,
     send_sems, recv_sems, own_sems,
 ):
     s, b, t = lax.axis_index("seq"), lax.axis_index("batch"), lax.axis_index("tp")
@@ -508,7 +508,7 @@
     same, other = s == c, s != c
 
     gate = pltpu.get_barrier_semaphore()
-    peers = [(s, 2 * yn + c, t), (sn, 2 * yn + c, t)]
+    peers = [(ds, 2 * yn + dc, t) for ds in range(2) for dc in range(2)]
     for ds in range(2):
         for dc in range(2):
             for dt in range(rows):
@@ -536,6 +536,10 @@
             for wire in group:
                 wire.start()
 
+    def sent_all(wires):
+        for wire in wires:
+            net.done(wire)
+
     def arrived_all(wires):
         for group in wires:
             for wire in group:
@@ -545,31 +549,12 @@
     bvec_wires = []
     for step in range(1, rows):
         bvec_wires.append(net.wire(bvec.at[0], bvec.at[step], dev(s, y, c, ring(-step))))
-    wa_z = []
-    for step in range(1, rows):
-        wa_z.append(net.wire(
-            wa_in.at[:, s, y], wa.at[:, lax.rem(t, 2), s, y], dev(s, y, c, ring(step)),
-            home, lax.div(ring(-step), 2) == c,
-        ))
     wa_own = net.own(wa_in, wa.at[:, lax.rem(t, 2)], home)
     token_wires = swap(tokens, x_own)
     wval_own = net.own(wval_in, wval, c == 0)
     lanes_c = pl.ds(pl.multiple_of(c * (wup.shape[-1]), 128), wup.shape[-1])
     up_own = net.own(wup_in.at[:, :, :, lanes_c], wup.at[0])
     down_own = net.own(wdown_in.at[c], wdown.at[0])
-
-    bvec[0] = bvec_in[...]
-    row_ids = lax.broadcasted_iota(jnp.int32, seg.shape, 0)
-    seg_row = jnp.sum(jnp.where(row_ids == t, seg[...], 0), axis=0, keepdims=True)
-    segint[0] = jnp.broadcast_to(seg_row, segint.shape[1:])
-    for wire in wa_z:
-        wire.start()
-    seg_wire.start()
-    for wire in bvec_wires:
-        wire.start()
-    start_all(token_wires)
-    for own in (wa_own, wval_own, up_own, down_own):
-        own.start()
 
     first_slot = net.recv_slots(2 * rows)
     first_wires = []
@@ -597,34 +582,112 @@
                     take()
         first_own.arrived()
 
-    up_z, down_z = [], []
-    for step in range(1, rows):
-        up_z.append(net.wire(wup_in.at[s, y, :, lanes_c], wup.at[step, s, y], dev(s, y, c, ring(-step))))
-        down_z.append(net.wire(wdown_in.at[c, s, y], wdown.at[step, s, y], dev(s, y, c, ring(-step))))
-    rest = pl.ds(1, rows - 1)
-    up_one = net.wire(wup.at[rest, s, y], wup.at[rest, s, y], x_nbr)
-    up_two = net.wire(wup.at[rest, :, y], wup.at[rest, :, y], y_nbr)
-    down_one = net.wire(wdown.at[rest, s, y], wdown.at[rest, s, y], y_nbr)
-    down_two = net.wire(wdown.at[rest, s], wdown.at[rest, s], x_nbr)
+    def along(own_piece, at_slot, only=None):
+        rounds = []
+        for r in range(1, rows):
+            pair = []
+            for right in (True, False):
+                source = t - (r - 1) if right else t + (r - 1)
+                came = t - r if right else t + r
+                inside = (source >= 0) & (t < rows - 1) if right else (source < rows) & (t > 0)
+                comes = came >= 0 if right else came < rows
+                if only is not None:
+                    inside, comes = inside & only(source), comes & only(came)
+                held = (rows - r + 1 if right else r - 1) % rows
+                lands = rows - r if right else r
+                src = own_piece if r == 1 else at_slot(source, held)
+                to = dev(s, y, c, jnp.minimum(t + 1, rows - 1) if right else jnp.maximum(t - 1, 0))
+                pair.append(net.wire(src, at_slot(source, lands), to, inside, comes))
+            rounds.append(pair)
+        return rounds
+
+    def heads_slot(source, step):
+        return wa.at[:, lax.rem(source + rows, 2), s, y]
+
+    wa_z = along(wa_in.at[:, s, y], heads_slot, lambda source: lax.div(source, 2) == c)
+    up_z = along(wup_in.at[s, y, :, lanes_c], lambda source, step: wup.at[step, s, y])
+    down_z = along(wdown_in.at[c, s, y], lambda source, step: wdown.at[step, s, y])
+
+    class Relay:
+        def __init__(self, k_, at_one, at_two, x_first, when=None):
+            self.k, self.when = k_, when
+            self.one = net.wire(at_one, at_one, x_nbr if x_first else y_nbr, when, when)
+            self.two = net.wire(at_two, at_two, y_nbr if x_first else x_nbr, when, when)
+
+        def at_round(self, r, act):
+            if r == self.k:
+                pl.when(t + self.k < rows)(act)
+            if r == rows - self.k:
+                pl.when(t + self.k >= rows)(act)
+
+        def first_hop(self, r):
+            self.at_round(r, self.one.start)
+
+        def second_hop(self, r):
+            def act():
+                self.one.arrived()
+                self.two.start()
+
+            self.at_round(r, act)
+
+    wa_relay, up_relay, down_relay = [], [], []
+    for k_ in range(1, rows):
+        source = ring(k_)
+        slot_of = lax.rem(source, 2)
+        wa_relay.append(Relay(
+            k_, wa.at[:, slot_of, s, y], wa.at[:, slot_of, :, y], True, lax.div(source, 2) == c,
+        ))
+        up_relay.append(Relay(k_, wup.at[k_, s, y], wup.at[k_, :, y], True))
+        down_relay.append(Relay(k_, wdown.at[k_, s, y], wdown.at[k_, s], False))
     cot_wires = swap(cot_in, cot.at[s])
     cot_mate = net.wire(cot.at[c], cot.at[c], mate)
 
-    wa_plane = []
-    for step in range(1, rows):
-        ours = lax.div(ring(-step), 2) == c
-        piece = wa.at[:, lax.rem(ring(-step), 2), s, y]
-        wa_plane.append([net.wire(piece, piece, to, ours, ours) for to in (x_nbr, y_nbr, diag)])
-    for step in range(1, rows):
-        wa_z[step - 1].arrived()
-        for wire in wa_plane[step - 1]:
+    bvec[0] = bvec_in[...]
+    row_ids = lax.broadcasted_iota(jnp.int32, seg.shape, 0)
+    seg_row = jnp.sum(jnp.where(row_ids == t, seg[...], 0), axis=0, keepdims=True)
+    segint[0] = jnp.broadcast_to(seg_row, segint.shape[1:])
+    for group in (wa_z[0], up_z[0], down_z[0]):
+        for wire in group:
             wire.start()
-
+    seg_wire.start()
+    for wire in bvec_wires:
+        wire.start()
+    for own in (wa_own, wval_own, up_own, down_own):
+        own.start()
+
+    paths = ((wa_z, wa_relay), (up_z, up_relay), (down_z, down_relay))
+
+    def hop(r):
+        for wires, relays in paths:
+            for wire in wires[r - 1]:
+                wire.arrived()
+            if r < rows - 1:
+                for wire in wires[r]:
+                    wire.start()
+            for relay in relays:
+                relay.first_hop(r)
+
+    def second_hop(r):
+        for _, relays in paths:
+            for relay in relays:
+                relay.second_hop(r)
+
+    hop(1)
+    hop(2)
+    start_all(token_wires)
+    second_hop(1)
     seg_wire.arrived()
     chosen = jnp.where(same, segint[0], segint[1]).astype(F4)
     segrow[...] = chosen
     for part in range(length // 128):
         piece = jnp.broadcast_to(chosen[0:1, part * 128:(part + 1) * 128], (128, 128))
         segcol[part * 128:(part + 1) * 128, :] = piece.T
+    hop(3)
+    second_hop(2)
+    sent_all([group[0] for group in token_wires[1:]])
+    for wire in first_wires:
+        wire.start()
+    first_own.start()
 
     n1_wires = []
     for step in range(rows):
@@ -636,14 +699,9 @@
         wire = net.wire(n1.at[c, place], n1.at[c, place], mate)
         wire.start()
         n1_wires.append(wire)
-    for wire in first_wires:
-        wire.start()
-    first_own.start()
-    for wire in up_z + down_z:
-        wire.start()
-    for group in wa_plane:
-        for wire in group:
-            wire.arrived()
+    second_hop(3)
+    for relay in wa_relay:
+        relay.two.arrived()
     wa_own.arrived()
     wval_own.arrived()
     for wire in bvec_wires:
@@ -675,6 +733,9 @@
         return carry
 
     lax.fori_loop(0, length // QB, project_in, 0)
+    sent_all(first_wires)
+    start_all(cot_wires)
+
 
     @pl.when(c == 0)
     def _():
@@ -723,25 +784,8 @@
         lax.fori_loop(0, pairs, pair, 0)
         lse[:, at] = lsecol[...].T[:lse.shape[0], :]
 
-    def relay_weights(stage):
-        if stage == 0:
-            for wire in up_z:
-                wire.arrived()
-            up_one.start()
-            for wire in down_z:
-                wire.arrived()
-            down_one.start()
-            start_all(cot_wires)
-        if stage == 1:
-            up_one.arrived()
-            up_two.start()
-            down_one.arrived()
-            down_two.start()
-
     def attention(bias, lsecol):
         for j in range(n_q):
-            if j == n_q - 1:
-                relay_weights(0)
             attend(j, bias, lsecol)
 
     pl.run_scoped(attention, pltpu.VMEM((QB, length), F4), pltpu.VMEM((QB, 128), F4))
@@ -776,105 +820,177 @@
         wire = net.wire(n2.at[c, i], n2.at[c, i], mate)
         wire.start()
         n2_wires.append(wire)
-    relay_weights(1)
-    arrived_all(cot_wires)
-    cot_mate.start()
     up_own.arrived()
     down_own.arrived()
-    up_two.arrived()
-    down_two.arrived()
+    for relay in up_relay + down_relay:
+        relay.two.arrived()
 
     hid = wup.shape[-1]
     back_wire = net.wire(xs.at[1], xr.at[1], mate)
     mlp_wire = net.wire(xs.at[2], xr.at[2], mate)
     out_wires = swap(out_s, out)
     gm_wires = [net.wire(gm.at[c, i], gm.at[c, i], mate) for i in range(rows)]
-    up_rs = (net.wire(gup.at[:, sn], up_r1, x_nbr), net.wire(gup.at[:, s, yn], up_r2, y_nbr))
-    down_rs = (net.wire(gdown.at[:, :, yn], down_r1, y_nbr), net.wire(gdown.at[:, sn, y], down_r2, x_nbr))
-    up_rz = [net.wire(gup.at[i, s, y], up_r3.at[i], dev(s, y, c, ring(i))) for i in range(1, rows)]
-    down_rz = [net.wire(gdown.at[i, s, y], down_r3.at[i], dev(s, y, c, ring(i))) for i in range(1, rows)]
+    order = tuple(range(1, rows)) + (0,)
+
+    class Reduce:
+        def __init__(self, grad, one, two, z, p, y_first):
+            self.grad, self.p, self.y_first = grad, p, y_first
+            self.got_one, self.got_two, self.z = one, two, None
+            if y_first:
+                self.one = net.wire(grad.at[p, :, yn], one.at[p], y_nbr)
+                self.two = net.wire(grad.at[p, sn, y], two.at[p], x_nbr)
+            else:
+                self.one = net.wire(grad.at[p, sn], one.at[p], x_nbr)
+                self.two = net.wire(grad.at[p, s, yn], two.at[p], y_nbr)
+            if p:
+                self.z = net.wire(grad.at[p, s, y], z.at[p], dev(s, y, c, ring(p)))
+
+        def run(self, stage):
+            grad, p = self.grad, self.p
+            if stage == 1:
+                self.one.arrived()
+                if self.y_first:
+                    grad[p, :, y] = add(grad[p, :, y], self.got_one[p])
+                else:
+                    grad[p, s] = add(grad[p, s], self.got_one[p])
+                self.two.start()
+            else:
+                self.two.arrived()
+                grad[p, s, y] = add(grad[p, s, y], self.got_two[p])
+                if p:
+                    self.z.start()
+
+    def add(one, two):
+        return (one.astype(F4) + two.astype(F4)).astype(BF)
+
+    down_rs = [Reduce(gdown, down_r1, down_r2, down_r3, p, True) for p in range(rows)]
+    up_rs = [Reduce(gup, up_r1, up_r2, up_r3, p, p < rows // 2) for p in range(rows)]
+
+    class Small:
+        def __init__(self, group):
+            self.group = group
+            self.here = 4 * s + 2 * y + c
+            mine_at = small_p.at[group, self.here]
+            self.plane = []
+            for ds in range(2):
+                for dy in range(2):
+                    for dc in range(2):
+                        if ds or dy or dc:
+                            to = dev(lax.rem(s + ds, 2), lax.rem(y + dy, 2), lax.rem(c + dc, 2), t)
+                            self.plane.append(net.wire(mine_at, mine_at, to))
+            at_z = small_z.at[group, t]
+            self.z = [net.wire(at_z, at_z, dev(s, y, c, ring(step))) for step in range(1, rows)]
+
+        def run(self, stage):
+            group = self.group
+            if stage == 0:
+                small_p[group, self.here] = small[group]
+                for wire in self.plane:
+                    wire.start()
+            elif stage == 1:
+                for wire in self.plane:
+                    wire.arrived()
+                total = small_p[group, 0]
+                for i in range(1, 8):
+                    total = total + small_p[group, i]
+                small_z[group, t] = total
+                for wire in self.z:
+                    wire.start()
+            else:
+                for wire in self.z:
+                    wire.arrived()
+                f_small[8 * group:8 * group + 8, :] = (
+                    (small_z[group, 0] + small_z[group, 1]) + (small_z[group, 2] + small_z[group, 3])
+                )
+
+    small_sums = [Small(0), Small(1)]
     gelu_scale = math.sqrt(2.0 / math.pi)
 
     def feed_forward(act, ghid, bup_sum, back_own):
         bup_sum[...] = jnp.zeros_like(bup_sum)
 
-        def block(h, i, keep):
+        def forward(h, i, keep):
             at = half_rows(h, i)
             n2_block = flat(n2[h, pl.ds(i * per_blk, per_blk)])
-            cot_block = flat(cot[h, pl.ds(i * per_blk, per_blk)])
-            mlp = back = None
+            mlp = None
             for p in range(rows):
                 cols = slice(p * hid, (p + 1) * hid)
-                w_u = flat(wup[p])
-                w_d = flat(wdown[p])
-                z = dot(n2_block, w_u) + bvec[p, 0:1, lanes_c]
+                z = dot(n2_block, flat(wup[p])) + bvec[p, 0:1, lanes_c]
                 z2 = z * z
                 th = jnp.tanh(gelu_scale * z * (1.0 + 0.044715 * z2))
                 cdf = 0.5 * (1.0 + th)
                 a = (z * cdf).astype(BF)
                 slope = cdf + 0.5 * z * (1.0 - th * th) * (gelu_scale * (1.0 + 3 * 0.044715 * z2))
                 act[at, cols] = a
-                part = dot(a, w_d)
+                ghid[at, cols] = slope.astype(BF)
+                part = dot(a, flat(wdown[p]))
                 mlp = part if mlp is None else mlp + part
-                g = (dot_nt(cot_block, w_d) * slope).astype(BF)
+            to = pl.ds(pl.multiple_of(i * QB, QB), QB)
+            if keep:
+                mine[to, :] = mlp
+            else:
+                xs[2, to, :] = mlp.astype(BF)
+
+        def backward(h, i, keep):
+            at = half_rows(h, i)
+            cot_block = flat(cot[h, pl.ds(i * per_blk, per_blk)])
+            back = None
+            for p in range(rows):
+                cols = slice(p * hid, (p + 1) * hid)
+                g = (dot_nt(cot_block, flat(wdown[p])) * ghid[at, cols].astype(F4)).astype(BF)
                 ghid[at, cols] = g
                 bup_sum[0:1, cols] += jnp.sum(g.astype(F4), axis=0, keepdims=True)
-                part = dot_nt(g, w_u)
+                part = dot_nt(g, flat(wup[p]))
                 back = part if back is None else back + part
             to = pl.ds(pl.multiple_of(i * QB, QB), QB)
             if keep:
-                mine[to, :] = mlp
                 back_own[to, :] = back
             else:
-                xs[2, to, :] = mlp.astype(BF)
                 xs[1, to, :] = back.astype(BF)
 
-        def mine_block(i, carry):
-            block(c, i, True)
-            return carry
-
-        def mate_block(i, carry):
-            block(cn, i, False)
-            return carry
-
-        lax.fori_loop(0, per_half, mine_block, 0)
+        def each(step, h, keep):
+            def body(i, carry):
+                step(h, i, keep)
+                return carry
+
+            lax.fori_loop(0, per_half, body, 0)
+
+        each(forward, c, True)
         for wire in n2_wires:
             wire.arrived()
+        each(forward, cn, False)
+        mlp_wire.start()
+        arrived_all(cot_wires)
+        cot_mate.start()
+        each(backward, c, True)
+        mlp_wire.arrived()
+        for i in range(rows):
+            at = slice(i * blk, (i + 1) * blk)
+            out_s[i] = (mid[at, :] + mine[at, :] + xr[2, at, :].astype(F4) + vecs[5:6, :]).astype(BF)
+        start_all(out_wires)
         cot_mate.arrived()
-        lax.fori_loop(0, per_half, mate_block, 0)
+
+        for p in order:
+            got = dot_tn(act[:, p * hid:(p + 1) * hid], flat(cot[...]))
+            gdown[p] = got.astype(BF).reshape(gdown.shape[1:])
+            down_rs[p].one.start()
+        each(backward, cn, False)
         back_wire.start()
-        mlp_wire.start()
-
-        def down_grad(p, carry):
-            cols = pl.ds(pl.multiple_of(p * hid, 128), hid)
-            got = dot_tn(act[:, cols], flat(cot[...]))
-            gdown[p] = got.astype(BF).reshape(gdown.shape[1:])
-            return carry
-
-        lax.fori_loop(0, rows, down_grad, 0)
-        down_rs[0].start()
-
-        def up_grad(p, carry):
-            cols = pl.ds(pl.multiple_of(p * hid, 128), hid)
+        for p in order:
             for m in range(2):
                 n2_part = flat(n2[:, :, :, m * (width // 2):(m + 1) * (width // 2)])
-                got = dot_tn(n2_part, ghid[:, cols])
+                got = dot_tn(n2_part, ghid[:, p * hid:(p + 1) * hid])
                 gup[p, m] = got.astype(BF).reshape(gup.shape[2:])
-            return carry
-
-        lax.fori_loop(0, rows, up_grad, 0)
-        up_rs[0].start()
-        small[0] = jnp.zeros(small.shape[1:], F4)
+            up_rs[p].one.start()
+        small[...] = jnp.zeros_like(small)
         for p in range(rows):
-            small[0, pl.ds(8 + ring(p), 1), lanes_c] = bup_sum[0:1, p * hid:(p + 1) * hid]
+            small[1, pl.ds(ring(p), 1), lanes_c] = bup_sum[0:1, p * hid:(p + 1) * hid]
 
         back_wire.arrived()
-        mlp_wire.arrived()
         sums = [jnp.zeros((1, width), F4) for _ in range(4)]
         for i in range(rows):
             at = slice(i * blk, (i + 1) * blk)
             middle = mid[at, :]
-            out_s[i] = (middle + mine[at, :] + xr[2, at, :].astype(F4) + vecs[5:6, :]).astype(BF)
             unit, inverse = norm_stats(middle)
             back = back_own[at, :] + xr[1, at, :].astype(F4)
             cot_block = cot[c, i].astype(F4)
@@ -886,8 +1002,8 @@
             for n, item in enumerate((back * unit, back, g_low.astype(F4), cot_block)):
                 sums[n] += jnp.sum(item, axis=0, keepdims=True)
         for n in range(4):
-            small[0, 2 + n:3 + n, :] = sums[n]
-        start_all(out_wires)
+            small[1, 4 + n:5 + n, :] = sums[n]
+        small_sums[1].run(0)
 
     pl.run_scoped(
         feed_forward,
@@ -897,70 +1013,36 @@
         pltpu.VMEM((half, width), F4),
     )
 
-    up_own_f = net.own(f_s.at[0], f_up.at[s, y, :, lanes_c])
-    up_ag = (
-        net.wire(f_s.at[0], f_up.at[s, y, :, lanes_c], x_nbr),
-        net.wire(f_up.at[:, y, :, lanes_c], f_up.at[:, y, :, lanes_c], y_nbr),
-        net.wire(f_up.at[:, :, :, lanes_c], f_up.at[:, :, :, lanes_c], mate),
-    )
-    down_own_f = net.own(f_t, f_down.at[c, s, y])
-    down_ag = (
-        net.wire(f_t, f_down.at[c, s, y], y_nbr),
-        net.wire(f_down.at[c, s], f_down.at[c, s], x_nbr),
-        net.wire(f_down.at[c], f_down.at[c], mate),
-    )
-
-    def add(one, two):
-        return (one.astype(F4) + two.astype(F4)).astype(BF)
-
-    def ffn_reduce(stage):
-        if stage == 0:
-            down_rs[0].arrived()
-            up_rs[0].arrived()
-
-            def one(p, carry):
-                gdown[p, :, y] = add(gdown[p, :, y], down_r1[p])
-                gup[p, s] = add(gup[p, s], up_r1[p])
-                return carry
-
-            lax.fori_loop(0, rows, one, 0)
-            down_rs[1].start()
-            up_rs[1].start()
-        if stage == 1:
-            down_rs[1].arrived()
-            up_rs[1].arrived()
-
-            def two(p, carry):
-                gdown[p, s, y] = add(gdown[p, s, y], down_r2[p])
-                gup[p, s, y] = add(gup[p, s, y], up_r2[p])
-                return carry
-
-            lax.fori_loop(0, rows, two, 0)
-            for wire in down_rz + up_rz:
-                wire.start()
-        if stage == 2:
-            for wire in down_rz + up_rz:
-                wire.arrived()
-            for to, kept, got in ((f_s.at[0], gup[0, s, y], up_r3), (f_t, gdown[0, s, y], down_r3)):
-                total = kept.astype(F4)
-                for i in range(1, rows):
-                    total += got[i].astype(F4)
-                to[...] = total.astype(BF)
-            for wire in (up_own_f, down_own_f, up_ag[0], down_ag[0]):
-                wire.start()
-        if stage == 3:
-            for wire in (up_own_f, down_own_f, up_ag[0], down_ag[0]):
-                wire.arrived()
-            up_ag[1].start()
-            down_ag[1].start()
-        if stage == 4:
-            up_ag[1].arrived()
-            down_ag[1].arrived()
-            up_ag[2].start()
-            down_ag[2].start()
-        if stage == 5:
-            up_ag[2].arrived()
-            down_ag[2].arrived()
+    plane = ((x_nbr, sn, y), (y_nbr, s, yn), (diag, sn, yn))
+
+    class Gather:
+        def __init__(self, parts, grad, got, total, at_own, at_core):
+            self.parts, self.grad, self.got, self.total = parts, grad, got, total
+            self.keep = net.own(total, at_own)
+            self.ag = [net.wire(total, at_own, to) for to, _, _ in plane]
+            self.over = net.wire(at_core, at_core, mate)
+
+        def run(self, stage):
+            if stage == 0:
+                for p in range(1, rows):
+                    self.parts[p].z.arrived()
+                total = self.grad[0, s, y].astype(F4)
+                for p in range(1, rows):
+                    total += self.got[p].astype(F4)
+                self.total[...] = total.astype(BF)
+                self.keep.start()
+                for wire in self.ag:
+                    wire.start()
+            elif stage == 1:
+                self.keep.arrived()
+                for wire in self.ag:
+                    wire.arrived()
+                self.over.start()
+            else:
+                self.over.arrived()
+
+    up_end = Gather(up_rs, gup, up_r3, f_s.at[0], f_up.at[s, y, :, lanes_c], f_up.at[:, :, :, lanes_c])
+    down_end = Gather(down_rs, gdown, down_r3, f_t, f_down.at[c, s, y], f_down.at[c])
 
     back1_wire = net.wire(xs.at[0], xr.at[0], mate)
     gtok_wires = swap(out_s, gtok)
@@ -975,52 +1057,108 @@
                 gv_s.at[h * rows + j], gfirst.at[t], dev(h, y, s, j), fine, None, gfirst_slot + step,
             ))
     gfirst_own = net.own(gv_s.at[rows + t], gfirst.at[t], (c == 1) & (s == 1))
-    wa_rs = (net.wire(gwa.at[:, :, sn], wa_r1, x_nbr), net.wire(gwa.at[:, :, s, yn], wa_r2, y_nbr))
-    wa_rz = []
-    for step in range(1, rows):
-        to = ring(step)
-        wa_rz.append(net.wire(
-            gwa.at[:, lax.rem(to, 2), s, y], wa_r3.at[step], dev(s, y, c, to), lax.div(to, 2) == c, home,
-        ))
-    wa_own_f = net.own(f_w, f_wa.at[:, s, y], home)
-    wa_ag = (
-        net.wire(f_w, f_wa.at[:, s, y], x_nbr, home, home),
-        net.wire(f_wa.at[:, :, y], f_wa.at[:, :, y], y_nbr, home, home),
-        net.wire(f_wa, f_wa, mate, home, away),
-    )
+    class Heads:
+        def __init__(self, first_one, count, x_first):
+            self.part = part = pl.ds(first_one, count)
+            self.x_first = x_first
+            if x_first:
+                self.one = net.wire(gwa.at[part, :, sn], wa_r1.at[part], x_nbr)
+                self.two = net.wire(gwa.at[part, :, s, yn], wa_r2.at[part], y_nbr)
+            else:
+                self.one = net.wire(gwa.at[part, :, :, yn], wa_r1.at[part], y_nbr)
+                self.two = net.wire(gwa.at[part, :, sn, y], wa_r2.at[part], x_nbr)
+            self.rz = []
+            for step in range(1, rows):
+                to = ring(step)
+                self.rz.append(net.wire(
+                    gwa.at[part, lax.rem(to, 2), s, y], wa_r3.at[step, part], dev(s, y, c, to),
+                    lax.div(to, 2) == c, home,
+                ))
+            self.keep = net.own(f_w.at[part], f_wa.at[part, s, y], home)
+            self.ag = [net.wire(f_w.at[part], f_wa.at[part, s, y], to, home, home) for to, _, _ in plane]
+            self.over = net.wire(f_wa.at[part], f_wa.at[part], mate, home, away)
+
+        def run(self, stage):
+            part = self.part
+            if stage == 0:
+                self.one.start()
+            elif stage == 0.5:
+                self.one.arrived()
+                if self.x_first:
+                    gwa[part, :, s] = add(gwa[part, :, s], wa_r1[part])
+                else:
+                    gwa[part, :, :, y] = add(gwa[part, :, :, y], wa_r1[part])
+                self.two.start()
+            elif stage == 1:
+                self.two.arrived()
+                gwa[part, :, s, y] = add(gwa[part, :, s, y], wa_r2[part])
+                for wire in self.rz:
+                    wire.start()
+            elif stage == 2:
+                @pl.when(home)
+                def _():
+                    for wire in self.rz:
+                        wire.copy.wait_recv()
+                    total = gwa[part, lax.rem(t, 2), s, y].astype(F4)
+                    for i in range(1, rows):
+                        total += wa_r3[i, part].astype(F4)
+                    f_w[part] = total.astype(BF)
+
+                self.keep.start()
+                for wire in self.ag:
+                    wire.start()
+            elif stage == 3:
+                self.keep.arrived()
+                for wire in self.ag:
+                    wire.arrived()
+                self.over.start()
+            else:
+                self.over.arrived()
+
+    heads_out, heads_q, heads_k = Heads(2, 1, False), Heads(0, 1, True), Heads(1, 1, False)
     lead, follow = c == 0, c == 1
-    wv_rs = (
-        net.wire(gwv.at[sn], wv_r1, x_nbr, lead, lead),
-        net.wire(gwv.at[s, yn], wv_r2, y_nbr, lead, lead),
-    )
+    wv_rs = [net.wire(gwv.at[ds, dy], wv_r1.at[i], to, lead, lead) for i, (to, ds, dy) in enumerate(plane)]
     wv_rz = [
         net.wire(wv_r3.at[t], wv_r3.at[t], dev(s, y, c, ring(step)), lead, lead) for step in range(1, rows)
     ]
     wv_own_f = net.own(f_v, f_wv.at[s, y], lead)
-    wv_ag = (
-        net.wire(f_v, f_wv.at[s, y], x_nbr, lead, lead),
-        net.wire(f_wv.at[:, y], f_wv.at[:, y], y_nbr, lead, lead),
-        net.wire(f_wv, f_wv, mate, lead, follow),
-    )
-    small_ar = [net.wire(small.at[i], small_r.at[i], to) for i, to in enumerate((mate, x_nbr, y_nbr))]
-    small_rz = [net.wire(small_z.at[t], small_z.at[t], dev(s, y, c, ring(step))) for step in range(1, rows)]
-
-    def small_reduce(stage):
+    wv_ag = [net.wire(f_v, f_wv.at[s, y], to, lead, lead) for to, _, _ in plane]
+    wv_over = net.wire(f_wv, f_wv, mate, lead, follow)
+
+    def fresh_reduce(stage):
         if stage == 0:
-            small_ar[0].start()
-        elif stage < 3:
-            small_ar[stage - 1].arrived()
-            small[stage] = small[stage - 1] + small_r[stage - 1]
-            small_ar[stage].start()
+            for wire in wv_rs:
+                wire.start()
+        elif stage == 1:
+            @pl.when(lead)
+            def _():
+                for wire in wv_rs:
+                    wire.copy.wait_recv()
+                total = gwv[s, y].astype(F4)
+                for i in range(3):
+                    total += wv_r1[i].astype(F4)
+                wv_r3[t] = total.astype(BF)
+
+            for wire in wv_rz:
+                wire.start()
+        elif stage == 2:
+            @pl.when(lead)
+            def _():
+                for wire in wv_rz:
+                    wire.copy.wait_recv()
+                parts = [wv_r3[i].astype(F4) for i in range(rows)]
+                f_v[...] = ((parts[0] + parts[1]) + (parts[2] + parts[3])).astype(BF)
+
+            wv_own_f.start()
+            for wire in wv_ag:
+                wire.start()
         elif stage == 3:
-            small_ar[2].arrived()
-            small_z[t] = small[2] + small_r[2]
-            for wire in small_rz:
-                wire.start()
+            wv_own_f.arrived()
+            for wire in wv_ag:
+                wire.arrived()
+            wv_over.start()
         else:
-            for wire in small_rz:
-                wire.arrived()
-            f_small[...] = (small_z[0] + small_z[1]) + (small_z[2] + small_z[3])
+            wv_over.arrived()
 
     heads_here = heads_width // HEAD_DIM
     pick_head = lax.broadcasted_iota(jnp.int32, (lse.shape[0], heads_width), 1) // HEAD_DIM
@@ -1054,6 +1192,9 @@
             wire.arrived()
         lax.fori_loop(0, per_half, grad_att_mate, 0)
         gwa[2] = dot_tn(att[...], flat(gm[...])).astype(BF).reshape(gwa.shape[1:])
+        heads_out.run(0)
+        down_rs[1].run(1)
+        down_rs[2].run(1)
 
         def back_block(j):
             count = (j + 1) * QB
@@ -1090,44 +1231,35 @@
 
         for j in range(n_q):
             back_block(j)
-            if j >= 1:
-                ffn_reduce(j - 1)
+            if j == 1:
+                down_rs[3].run(1)
+                up_rs[2].run(1)
+            if j == 2:
+                down_rs[0].run(1)
+                up_rs[3].run(1)
+                down_rs[1].run(2)
+                down_rs[2].run(2)
+            if j == 3:
+                up_rs[1].run(1)
+                down_rs[3].run(2)
+                up_rs[2].run(2)
+                up_rs[3].run(2)
 
         gq[...] = gqt[...].T
         gk_low = gk[...].astype(BF)
         k[...] = gk_low
         gv_s[...] = gv[...].astype(BF).reshape(gv_s.shape)
 
-        def back_rows(h, i):
-            at = half_rows(h, i)
-            tmp[...] = dot(gq[at, :], flat(wq[...])) + dot(k[at, :], flat(wk[...]))
-
-            @pl.when(lead)
-            def _():
-                block = flat(gv_s[pl.ds(h * rows + i * per_blk, per_blk)])
-                tmp[...] += dot_nt(block, wval[...])
-
-        def back_mate(i, carry):
-            back_rows(cn, i)
-            xs[0, pl.ds(pl.multiple_of(i * QB, QB), QB), :] = tmp[...].astype(BF)
-            return carry
-
-        def back_mine(i, carry):
-            back_rows(c, i)
-            mine[pl.ds(pl.multiple_of(i * QB, QB), QB), :] = tmp[...]
-            return carry
-
-        net.done(att_wire)
-        lax.fori_loop(0, per_half, back_mate, 0)
-        back1_wire.start()
+        n1_all = flat(n1[...])
+        gwa[0] = dot(gqt[...], n1_all).astype(BF).reshape(gwa.shape[1:])
+        heads_q.run(0)
+        gwa[1] = dot_tn(k[...], n1_all).astype(BF).reshape(gwa.shape[1:])
+        heads_k.run(0)
         for wire in gfirst_wires:
             wire.start()
         gfirst_own.start()
-        lax.fori_loop(0, per_half, back_mine, 0)
-        n1_all = flat(n1[...])
-        gwa[0] = dot(gqt[...], n1_all).astype(BF).reshape(gwa.shape[1:])
-        gwa[1] = dot_tn(k[...], n1_all).astype(BF).reshape(gwa.shape[1:])
-        wa_rs[0].start()
+        up_rs[0].run(1)
+        down_rs[0].run(2)
         small[0, 7:8, lanes_h] = jnp.sum(gq[...].astype(F4), axis=0, keepdims=True)
 
         @pl.when(lead)
@@ -1136,7 +1268,34 @@
             gwv[...] = dot_tn(gv_low, n1_all).astype(BF).reshape(gwv.shape)
             small[0, 6:7, :heads_width] = jnp.sum(gv_low.astype(F4), axis=0, keepdims=True)
 
-        wv_rs[0].start()
+        fresh_reduce(0)
+        heads_out.run(0.5)
+        small_sums[1].run(1)
+
+        def back_rows(h, i):
+            at = half_rows(h, i)
+            tmp[...] = dot(gq[at, :], flat(wq[...])) + dot(k[at, :], flat(wk[...]))
+
+            @pl.when(lead)
+            def _():
+                block = flat(gv_s[pl.ds(h * rows + i * per_blk, per_blk)])
+                tmp[...] += dot_nt(block, wval[...])
+
+        def back_mate(i, carry):
+            back_rows(cn, i)
+            xs[0, pl.ds(pl.multiple_of(i * QB, QB), QB), :] = tmp[...].astype(BF)
+            return carry
+
+        def back_mine(i, carry):
+            back_rows(c, i)
+            mine[pl.ds(pl.multiple_of(i * QB, QB), QB), :] = tmp[...]
+            return carry
+
+        net.done(att_wire)
+        lax.fori_loop(0, per_half, back_mate, 0)
+        back1_wire.start()
+        lax.fori_loop(0, per_half, back_mine, 0)
+        up_rs[1].run(2)
 
     lanes_h = pl.ds(pl.multiple_of(c * heads_width, 128), heads_width)
     pl.run_scoped(
@@ -1167,66 +1326,36 @@
     small[0, 0:1, :] = gain_sum
     small[0, 1:2, :] = bias_sum
     start_all(gtok_wires)
-    small_reduce(0)
-
-    wa_rs[0].arrived()
-    gwa[:, :, s] = add(gwa[:, :, s], wa_r1[...])
-    wa_rs[1].start()
-
-    @pl.when(lead)
-    def _():
-        wv_rs[0].copy.wait_recv()
-        gwv[s] = add(gwv[s], wv_r1[...])
-        wv_rs[1].copy.start()
-
-    small_reduce(1)
-    ffn_reduce(3)
-    small_reduce(2)
-    wa_rs[1].arrived()
-    gwa[:, :, s, y] = add(gwa[:, :, s, y], wa_r2[...])
-    for wire in wa_rz:
-        wire.start()
-
-    @pl.when(lead)
-    def _():
-        wv_rs[1].copy.wait_recv()
-        wv_r3[t] = add(gwv[s, y], wv_r2[...])
-        for wire in wv_rz:
-            wire.copy.start()
-
-    small_reduce(3)
-    ffn_reduce(4)
-
-    @pl.when(home)
-    def _():
-        for wire in wa_rz:
-            wire.copy.wait_recv()
-        total = gwa[:, lax.rem(t, 2), s, y].astype(F4)
-        for i in range(1, rows):
-            total += wa_r3[i].astype(F4)
-        f_w[...] = total.astype(BF)
-
-    wa_own_f.start()
-    wa_ag[0].start()
-
-    @pl.when(lead)
-    def _():
-        for wire in wv_rz:
-            wire.copy.wait_recv()
-        parts = [wv_r3[i].astype(F4) for i in range(rows)]
-        f_v[...] = ((parts[0] + parts[1]) + (parts[2] + parts[3])).astype(BF)
-
-    wv_own_f.start()
-    wv_ag[0].start()
-    small_reduce(4)
-    for stage in range(2):
-        for wire in ((wa_own_f, wv_own_f) if stage == 0 else ()) + (wa_ag[stage], wv_ag[stage]):
-            wire.arrived()
-        wa_ag[stage + 1].start()
-        wv_ag[stage + 1].start()
-    ffn_reduce(5)
-    wa_ag[2].arrived()
-    wv_ag[2].arrived()
+    small_sums[0].run(0)
+
+    heads_out.run(1)
+    up_rs[0].run(2)
+    down_end.run(0)
+    heads_q.run(0.5)
+    heads_k.run(0.5)
+    fresh_reduce(1)
+    small_sums[0].run(1)
+    heads_q.run(1)
+    heads_k.run(1)
+    heads_out.run(2)
+    up_end.run(0)
+    down_end.run(1)
+    fresh_reduce(2)
+    heads_q.run(2)
+    heads_k.run(2)
+    heads_out.run(3)
+    up_end.run(1)
+    fresh_reduce(3)
+    heads_q.run(3)
+    heads_k.run(3)
+    small_sums[1].run(2)
+    small_sums[0].run(2)
+    down_end.run(2)
+    up_end.run(2)
+    heads_out.run(4)
+    heads_q.run(4)
+    heads_k.run(4)
+    fresh_reduce(4)
     for group in out_wires:
         group[0].arrived()
     arrived_all(gtok_wires)
@@ -1295,8 +1424,8 @@
         room(rows, 2, up_rows, hid), room(rows, up_rows, hid), room(rows, up_rows, hid),
         room(rows, 2, down_rows, width), room(rows, down_rows, width), room(rows, down_rows, width),
         room(3, 2, 2, 2, piece, width), room(3, 2, 2, piece, width), room(3, 2, piece, width), room(rows, 3, piece, width),
-        room(2, 2, valf // 4, width), room(2, valf // 4, width), room(valf // 4, width), room(rows, valf // 4, width),
-        room(3, 16, width, dtype=F4), room(3, 16, width, dtype=F4), room(rows, 16, width, dtype=F4),
+        room(2, 2, valf // 4, width), room(3, valf // 4, width), room(rows, valf // 4, width),
+        room(2, 8, width, dtype=F4), room(2, 8, 8, width, dtype=F4), room(2, rows, 8, width, dtype=F4),
         room(1, up_rows, hid), room(down_rows, width), room(3, piece, width), room(valf // 4, width),
         pltpu.SemaphoreType.DMA((SENDS,)), pltpu.SemaphoreType.DMA((RECVS,)), pltpu.SemaphoreType.DMA((OWNS,)),
     ]
@@ -1328,18 +1457,18 @@
         f_wv.reshape(valf, width).astype(F4).T,
         f_small[6, :valf],
         wa_flat[2],
-        f_small[4],
-        f_small[2],
-        f_small[3],
+        f_small[14],
+        f_small[12],
+        f_small[13],
         f_up.reshape(width, 2 * hid).astype(F4),
         grad_b_up,
         f_down.reshape(2 * hid, width).astype(F4),
-        f_small[5],
-    )
-
-
-SENDS = 120
-RECVS = 120
+        f_small[15],
+    )
+
+
+SENDS = 176
+RECVS = 176
 OWNS = 16
 VMEM_BYTES = 63 * 1024 * 1024
 

time: 311 us -> 243 us (0.78)
  Pallas kernels: 289 us -> 219 us
    pallas_call x1, Pallas kernels: 289 us -> 219 us  [whole_layer(): pl.pallas_call(layer_kernel, out_shape=outs, in_specs=[hbm, hbm, hbm, vme...]
where the time goes in v2:
time: 243 us; the launch traced here: 239 us
  Pallas kernels  219 us (90%)
  local copies, waits for them, and re-layouts  11.3 us (5%)
  other arithmetic  8.35 us (3%)
    pallas_call x1, Pallas kernels, whole_layer(): pl.pallas_call(layer_kernel, out_shape=outs, in_specs=[hbm, hbm, hbm, vme...  219 us

profile of v2, /device:TPU:1, one launch (start us, length us, event | category | flops | bytes accessed | tf_op | source)
XLA Modules:
  0.0 239.4 jit_solution(3721403129125108863)
XLA Ops:
  0.7 0.0 copy-start.12
  0.7 0.0 copy-start.6
  0.7 0.0 copy-start.7
  0.7 0.0 copy-start.8
  0.7 0.0 copy-start.9
  0.7 0.0 copy-start.10
  0.7 0.8 pad_select_fusion
  1.6 0.7 broadcast_in_dim.9
  2.3 0.1 pad.17.clone
  2.3 0.7 maximum_maximum_fusion.bvec_in
  3.0 2.1 pad_maximum_fusion.wa_in
  5.2 0.0 copy-done.12
  5.2 0.0 copy-done.6
  5.2 0.0 copy-done.8
  5.3 0.7 stack.47.vecs
  6.0 218.6 %shard_map.322 = (bf16[4,128,768]{2,1,0:T(8,128)(2,1)}, bf16[4,128,768]{2,1,0:T(8,128)(2,1)}, bf16[4,128,384]{2,1,0:T(8,128)(2,1)}, bf16[2,2,192,768]{3,2,1,0:T(...) custom-call(bf16[4,128,768]{2,1,0:T(8,128)(2,1)} %tokens.1, ...), custom_call_target="tpu_custom_call" | custom-call | tf_op jit(solution)/shard_map/pallas_call | solution.py:1432
  224.6 1.6 slice_reduce_fusion
  226.2 1.3 constant_dynamic-slice_fusion
  227.5 2.4 %fusion = (f32[1,2,2,48,768]{4,3,2,1,0:T(8,128)}, f32[1,2,2,48,768]{4,3,2,1,0:T(8,128)}, f32[1,2,2,48,768]{4,3,2,1,0:T(8,128)}) fusion(bf16[3,2,2,48,768]{4,3,2,1,0:T(8,128)(2,1)} %get-tuple-element.30), kind=kLoop, calls=%fused_computation.15 | loop fusion | bytes 3538944 | tf_op jit(solution)/shard_map/slice | solution.py:1459
  230.0 1.3 slice_reduce_fusion.6
  231.3 0.0 copy-done.4
  231.3 0.1 bitcast_convert_fusion.2
  231.4 1.4 copy.37
  232.8 0.0 copy-done.1
  232.8 1.7 bitcast_convert_fusion
  234.4 0.0 copy-done
  234.4 1.7 bitcast_convert_fusion.1
  236.1 1.3 convert_element_type.29
  237.4 0.1 copy-done.2
  237.5 0.9 copy.40
  238.3 0.0 copy-done.5
  238.4 0.7 copy.41
  (23 shorter events, 0.1 us)
Async XLA Ops:
  0.7 4.5 %copy-start.12 = (f32[384]{0:T(512)S(1)}, f32[384]{0:T(512)}, u32[]{:S(2)}) copy-start(f32[384]{0:T(512)} %param.29) | copy-start | bytes 4612
  0.7 4.5 %copy-start.6 = (f32[768]{0:T(1024)S(1)}, f32[768]{0:T(1024)}, u32[]{:S(2)}) copy-start(f32[768]{0:T(1024)} %param.23) | copy-start | bytes 9220
  0.7 4.5 %copy-start.7 = (f32[768]{0:T(1024)S(1)}, f32[768]{0:T(1024)}, u32[]{:S(2)}) copy-start(f32[768]{0:T(1024)} %param.24) | copy-start | bytes 9220
  0.7 4.5 %copy-start.8 = (f32[768]{0:T(1024)S(1)}, f32[768]{0:T(1024)}, u32[]{:S(2)}) copy-start(f32[768]{0:T(1024)} %param.32) | copy-start | bytes 9220
  0.7 4.6 %copy-start.9 = (f32[768]{0:T(1024)S(1)}, f32[768]{0:T(1024)}, u32[]{:S(2)}) copy-start(f32[768]{0:T(1024)} %param.33) | copy-start | bytes 9220
  0.7 4.6 %copy-start.10 = (f32[768]{0:T(1024)S(1)}, f32[768]{0:T(1024)}, u32[]{:S(2)}) copy-start(f32[768]{0:T(1024)} %param.31) | copy-start | bytes 9220
  0.7 4.6 %copy-start.11 = (f32[768]{0:T(1024)S(1)}, f32[768]{0:T(1024)}, u32[]{:S(2)}) copy-start(f32[768]{0:T(1024)} %param.37) | copy-start | bytes 9220
  227.5 3.8 %copy-start.4 = (bf16[2,2,96,768]{3,2,1,0:T(8,128)(2,1)S(1)}, bf16[2,2,96,768]{3,2,1,0:T(8,128)(2,1)}, u32[]{:S(2)}) copy-start(bf16[2,2,96,768]{3,2,1,0:T(8,128)(2,1)} %get-tuple-element.31) | copy-start | bytes 1769476
  231.4 1.4 copy-start.1
  232.8 1.7 copy-start
  234.4 1.7 copy-start.3
  236.1 1.4 copy-start.2
  237.4 1.0 copy-start.5

commit v3 on v2

--- a/solution.py
+++ b/solution.py
@@ -478,9 +478,10 @@
 
 
 def layer_kernel(
-    tokens, first, cot_in, seg, wa_in, wup_in, wdown_in, wval_in, bvec_in, vecs,
+    tokens, first, cot_in, seg, wq_in, wk_in, wo_in, wup_in, wdown_in, wval_in,
+    gain1, bias1, gain2, bias2, b_out, b_down, b_value, b_query, b_up,
     out, gtok, gfirst, f_up, f_down, f_wa, f_wv, f_small,
-    x_own, n1, segint, segrow, segcol, bvec, wa, wval, wup, wdown,
+    x_own, n1, segint, segrow, segcol, vecs, bvec, wa, wval, wup, wdown,
     q, k, v, att, lse, mid, n2, cot,
     mine, xs, xr, out_s, gm, gatt, gv_s,
     gup, gdown, up_r1, up_r2, up_r3, down_r1, down_r2, down_r3,
@@ -507,6 +508,10 @@
     away = lax.div(t, 2) != c
     same, other = s == c, s != c
 
+    wa_own = [net.own(src, wa.at[i, lax.rem(t, 2)], home) for i, src in enumerate((wq_in, wk_in, wo_in))]
+    for own in wa_own:
+        own.start()
+
     gate = pltpu.get_barrier_semaphore()
     peers = [(ds, 2 * yn + dc, t) for ds in range(2) for dc in range(2)]
     for ds in range(2):
@@ -549,7 +554,6 @@
     bvec_wires = []
     for step in range(1, rows):
         bvec_wires.append(net.wire(bvec.at[0], bvec.at[step], dev(s, y, c, ring(-step))))
-    wa_own = net.own(wa_in, wa.at[:, lax.rem(t, 2)], home)
     token_wires = swap(tokens, x_own)
     wval_own = net.own(wval_in, wval, c == 0)
     lanes_c = pl.ds(pl.multiple_of(c * (wup.shape[-1]), 128), wup.shape[-1])
@@ -604,7 +608,7 @@
     def heads_slot(source, step):
         return wa.at[:, lax.rem(source + rows, 2), s, y]
 
-    wa_z = along(wa_in.at[:, s, y], heads_slot, lambda source: lax.div(source, 2) == c)
+    wa_z = along(wa.at[:, lax.rem(t, 2), s, y], heads_slot, lambda source: lax.div(source, 2) == c)
     up_z = along(wup_in.at[s, y, :, lanes_c], lambda source, step: wup.at[step, s, y])
     down_z = along(wdown_in.at[c, s, y], lambda source, step: wdown.at[step, s, y])
 
@@ -642,17 +646,32 @@
     cot_wires = swap(cot_in, cot.at[s])
     cot_mate = net.wire(cot.at[c], cot.at[c], mate)
 
-    bvec[0] = bvec_in[...]
+    bvec[0] = jnp.zeros(bvec.shape[1:], F4)
+    bvec[0, 0:1, :] = b_up[...].reshape(1, width)
+    shard = b_query.shape[0]
+
+    @pl.when(lax.rem(t, 2) == 0)
+    def _():
+        bvec[0, 1:2, :shard] = b_query[...].reshape(1, shard)
+
+    @pl.when(lax.rem(t, 2) == 1)
+    def _():
+        bvec[0, 1:2, shard:2 * shard] = b_query[...].reshape(1, shard)
+
+    for i, vector in enumerate((gain1, bias1, gain2, bias2, b_out, b_down, b_value)):
+        vecs[i:i + 1, :vector.shape[0]] = vector[...].reshape(1, vector.shape[0])
     row_ids = lax.broadcasted_iota(jnp.int32, seg.shape, 0)
     seg_row = jnp.sum(jnp.where(row_ids == t, seg[...], 0), axis=0, keepdims=True)
     segint[0] = jnp.broadcast_to(seg_row, segint.shape[1:])
+    for own in wa_own:
+        own.arrived()
     for group in (wa_z[0], up_z[0], down_z[0]):
         for wire in group:
             wire.start()
     seg_wire.start()
     for wire in bvec_wires:
         wire.start()
-    for own in (wa_own, wval_own, up_own, down_own):
+    for own in (wval_own, up_own, down_own):
         own.start()
 
     paths = ((wa_z, wa_relay), (up_z, up_relay), (down_z, down_relay))
@@ -702,7 +721,6 @@
     second_hop(3)
     for relay in wa_relay:
         relay.two.arrived()
-    wa_own.arrived()
     wval_own.arrived()
     for wire in bvec_wires:
         wire.arrived()
@@ -864,7 +882,7 @@
         return (one.astype(F4) + two.astype(F4)).astype(BF)
 
     down_rs = [Reduce(gdown, down_r1, down_r2, down_r3, p, True) for p in range(rows)]
-    up_rs = [Reduce(gup, up_r1, up_r2, up_r3, p, p < rows // 2) for p in range(rows)]
+    up_rs = [Reduce(gup, up_r1, up_r2, up_r3, p, p == 0) for p in range(rows)]
 
     class Small:
         def __init__(self, group):
@@ -1384,15 +1402,7 @@
     valf = w_value.shape[1]
     tp_width = w_query.shape[1]
     hid = w_up.shape[1] // 2
-    t = lax.axis_index("tp")
-    wa_in = jnp.stack([w_query.T, w_key.T, w_out]).reshape(3, 2, 2, tp_width // 4, width)
-    odd = lax.rem(t, 2) == 1
-    b_q = jnp.where(odd, jnp.pad(b_query, (tp_width, width - 2 * tp_width)), jnp.pad(b_query, (0, width - tp_width)))
-    bvec = jnp.concatenate([b_up[None], b_q[None], jnp.zeros((6, width), F4)])
-    vecs = jnp.stack([
-        norm1_gain, norm1_bias, norm2_gain, norm2_bias, b_out, b_down,
-        jnp.pad(b_value, (0, width - valf)), jnp.zeros((width,), F4),
-    ])
+    heads = tuple(w.reshape(2, 2, tp_width // 4, width) for w in (w_query.T, w_key.T, w_out))
     hbm = pl.BlockSpec(memory_space=pl.ANY)
     vmem = pl.BlockSpec(memory_space=pltpu.VMEM)
     piece = tp_width // 4
@@ -1411,7 +1421,7 @@
     )
     scratch = [
         room(rows, blk, width), room(2, rows, blk, width), room(2, 8, length, dtype=jnp.int32),
-        room(8, length, dtype=F4), room(length, 128, dtype=F4), room(rows, 8, width, dtype=F4),
+        room(8, length, dtype=F4), room(length, 128, dtype=F4), room(8, width, dtype=F4), room(rows, 8, width, dtype=F4),
         room(3, 2, 2, 2, piece, width), room(width, valf),
         room(rows, 2, 2, up_rows, hid), room(rows, 2, 2, down_rows, width),
         room(length, 2 * tp_width), room(length, 2 * tp_width), room(2 * rows, blk, valf),
@@ -1432,44 +1442,106 @@
     out, gtok, gfirst, f_up, f_down, f_wa, f_wv, f_small = pl.pallas_call(
         layer_kernel,
         out_shape=outs,
-        in_specs=[hbm, hbm, hbm, vmem, hbm, hbm, hbm, hbm, vmem, vmem],
+        in_specs=[hbm, hbm, hbm, vmem] + [hbm] * 6 + [vmem] * 9,
         out_specs=(hbm,) * 7 + (vmem,),
         scratch_shapes=scratch,
         compiler_params=pltpu.CompilerParams(
             collective_id=0, has_side_effects=True, vmem_limit_bytes=VMEM_BYTES
         ),
     )(
-        tokens, first_values, cotangent, segment_ids, wa_in,
-        w_up.reshape(2, 2, up_rows, 2 * hid), w_down.reshape(2, 2, 2, down_rows, width), w_value, bvec, vecs,
-    )
-    wa_flat = f_wa.reshape(3, tp_width, width).astype(F4)
-    grad_b_query = lax.dynamic_slice(f_small, (7, t * tp_width), (1, tp_width))[0]
-    grad_b_up = lax.dynamic_slice(f_small, (8 + t, 0), (1, width))[0]
+        tokens, first_values, cotangent, segment_ids, *heads,
+        w_up.reshape(2, 2, up_rows, 2 * hid), w_down.reshape(2, 2, 2, down_rows, width), w_value,
+        norm1_gain, norm1_bias, norm2_gain, norm2_bias, b_out, b_down, b_value, b_query, b_up,
+    )
+    vector = of(width, dtype=F4)
+    results = pl.pallas_call(
+        finish_kernel,
+        out_shape=(
+            of(rows, blk, width), of(rows, blk, valf), of(rows, blk, width, dtype=F4),
+            of(width, 2 * hid, dtype=F4), of(2 * hid, width, dtype=F4),
+            of(tp_width, width, dtype=F4), of(tp_width, width, dtype=F4), of(tp_width, width, dtype=F4),
+            of(width, valf, dtype=F4),
+            vector, vector, vector, vector, vector, vector, of(valf, dtype=F4), of(tp_width, dtype=F4), vector,
+        ),
+        in_specs=[hbm] * 7 + [vmem],
+        out_specs=(hbm,) * 9 + (vmem,) * 9,
+        scratch_shapes=[
+            room(rows, blk, width), room(rows, blk, valf),
+            room(rows, blk, width), room(width, 2 * hid), room(2 * hid, width), room(3 * tp_width, width), room(valf, width),
+            room(rows, blk, width, dtype=F4), room(width, 2 * hid, dtype=F4), room(2 * hid, width, dtype=F4),
+            room(tp_width, width, dtype=F4), room(tp_width, width, dtype=F4), room(tp_width, width, dtype=F4),
+            room(width, valf, dtype=F4),
+            pltpu.SemaphoreType.DMA((7,)), pltpu.SemaphoreType.DMA((9,)),
+        ],
+        compiler_params=pltpu.CompilerParams(vmem_limit_bytes=VMEM_BYTES),
+    )(
+        out, gfirst, gtok, f_up.reshape(width, 2 * hid), f_down.reshape(2 * hid, width),
+        f_wa.reshape(3 * tp_width, width), f_wv.reshape(valf, width), f_small,
+    )
+    (out, gfirst, gtok, grad_up, grad_down, grad_q, grad_k, grad_o, grad_v,
+     gain1, bias1, gain2, bias2, grad_b_out, grad_b_down, grad_b_v, grad_b_q, grad_b_up) = results
     return (
-        out,
-        gtok.astype(F4),
-        gfirst,
-        f_small[0],
-        f_small[1],
-        wa_flat[0].T,
-        grad_b_query,
-        wa_flat[1].T,
-        f_wv.reshape(valf, width).astype(F4).T,
-        f_small[6, :valf],
-        wa_flat[2],
-        f_small[14],
-        f_small[12],
-        f_small[13],
-        f_up.reshape(width, 2 * hid).astype(F4),
-        grad_b_up,
-        f_down.reshape(2 * hid, width).astype(F4),
-        f_small[15],
-    )
+        out, gtok, gfirst, gain1, bias1, grad_q.T, grad_b_q, grad_k.T, grad_v, grad_b_v, grad_o, grad_b_out,
+        gain2, bias2, grad_up, grad_b_up, grad_down, grad_b_down,
+    )
+
+
+def finish_kernel(
+    out, gfirst, gtok, up, down, heads, value, small,
+    out_o, gfirst_o, gtok_o, up_o, down_o, q_o, k_o, o_o, value_o,
+    gain1, bias1, gain2, bias2, b_out, b_down, b_value, b_query, b_up,
+    out_i, gfirst_i, gtok_i, up_i, down_i, heads_i, value_i, gtok_f, up_f, down_f, q_f, k_f, o_f, value_f, in_sems, out_sems,
+):
+    t = lax.axis_index("tp")
+    loads = [
+        pltpu.make_async_copy(src, dst, in_sems.at[i])
+        for i, (src, dst) in enumerate((
+            (up, up_i), (down, down_i), (gtok, gtok_i), (heads, heads_i), (value, value_i), (out, out_i), (gfirst, gfirst_i),
+        ))
+    ]
+    for copy in loads:
+        copy.start()
+    stores = [
+        pltpu.make_async_copy(src, dst, out_sems.at[i])
+        for i, (src, dst) in enumerate((
+            (up_f, up_o), (down_f, down_o), (gtok_f, gtok_o), (q_f, q_o), (k_f, k_o), (o_f, o_o), (value_f, value_o),
+            (out_i, out_o), (gfirst_i, gfirst_o),
+        ))
+    ]
+    for row, ref in enumerate((gain1, bias1)):
+        ref[...] = small[row, :]
+    for row, ref in enumerate((gain2, bias2, b_out, b_down)):
+        ref[...] = small[12 + row, :]
+    b_value[...] = small[6, :b_value.shape[0]]
+    b_up[...] = small[8 + t, :]
+    shard = b_query.shape[0]
+    mine = jnp.zeros((1, shard), F4)
+    for i in range(small.shape[1] // shard):
+        mine = jnp.where(t == i, small[7:8, i * shard:(i + 1) * shard], mine)
+    b_query[...] = mine.reshape(shard)
+    for i, (src, dst) in enumerate(((up_i, up_f), (down_i, down_f), (gtok_i, gtok_f))):
+        loads[i].wait()
+        dst[...] = src[...].astype(F4)
+        stores[i].start()
+    loads[3].wait()
+    for i, ref in enumerate((q_f, k_f)):
+        ref[...] = heads_i[i * shard:(i + 1) * shard, :].astype(F4)
+        stores[3 + i].start()
+    o_f[...] = heads_i[2 * shard:3 * shard, :].astype(F4)
+    stores[5].start()
+    loads[4].wait()
+    value_f[...] = value_i[...].astype(F4).T
+    stores[6].start()
+    for i in range(2):
+        loads[5 + i].wait()
+        stores[7 + i].start()
+    for copy in stores:
+        copy.wait()
 
 
 SENDS = 176
 RECVS = 176
-OWNS = 16
+OWNS = 20
 VMEM_BYTES = 63 * 1024 * 1024
 
 

time: 243 us -> 228 us (0.938)
  local copies, waits for them, and re-layouts: 11.3 us -> 0 us
  other arithmetic: 8.35 us -> 0 us
  Pallas kernels: 219 us -> 225 us
    pallas_call x0 -> x1, Pallas kernels: none -> 6.89 us  [whole_layer(): pl.pallas_call(finish_kernel, out_shape=(of(rows, blk, width), of(rows, b...]
    slice x3 -> x0, local copies, waits for them, and re-layouts: 5.35 us -> none  [the longest x1 2.45 us: whole_layer(): wa_flat[2]]
    convert_element_type x3 -> x0, other arithmetic: 4.57 us -> none  [the longest x1 1.65 us: whole_layer(): f_up.reshape(width, 2 * hid).astype(F4)]
where the time goes in v3:
time: 228 us; the launch traced here: 226 us
  Pallas kernels  225 us (99%)
    pallas_call x1, Pallas kernels, whole_layer(): pl.pallas_call(layer_kernel, out_shape=outs, in_specs=[hbm, hbm, hbm, vme...  218 us
    pallas_call x1, Pallas kernels, whole_layer(): pl.pallas_call(finish_kernel, out_shape=(of(rows, blk, width), of(rows, b...  6.89 us

profile of v3, /device:TPU:1, one launch (start us, length us, event | category | flops | bytes accessed | tf_op | source)
XLA Modules:
  0.0 225.7 jit_solution(14331804959251562347)
XLA Ops:
  0.7 217.7 %shard_map.322 = (bf16[4,128,768]{2,1,0:T(8,128)(2,1)}, bf16[4,128,768]{2,1,0:T(8,128)(2,1)}, bf16[4,128,384]{2,1,0:T(8,128)(2,1)}, bf16[2,2,192,768]{3,2,1,0:T(...) custom-call(bf16[4,128,768]{2,1,0:T(8,128)(2,1)} %tokens.1, ...), custom_call_target="tpu_custom_call" | custom-call | tf_op jit(solution)/shard_map/pallas_call | solution.py:1442
  218.4 6.9 %shard_map.323 = (bf16[4,128,768]{2,1,0:T(8,128)(2,1)}, bf16[4,128,384]{2,1,0:T(8,128)(2,1)}, f32[4,128,768]{2,1,0:T(8,128)}, f32[768,768]{1,0:T(8,128)}, f32[76...) custom-call(bf16[4,128,768]{2,1,0:T(8,128)(2,1)} %get-tuple-element., ...), custom_call_target="tpu_custom_call" | custom-call | tf_op jit(solution)/shard_map/pallas_call | solution.py:1457

commit v4 on v3

--- a/solution.py
+++ b/solution.py
@@ -976,22 +976,22 @@
         each(forward, c, True)
         for wire in n2_wires:
             wire.arrived()
+        arrived_all(cot_wires)
+        cot_mate.start()
         each(forward, cn, False)
         mlp_wire.start()
-        arrived_all(cot_wires)
-        cot_mate.start()
+        cot_mate.arrived()
+
+        for p in order:
+            got = dot_tn(act[:, p * hid:(p + 1) * hid], flat(cot[...]))
+            gdown[p] = got.astype(BF).reshape(gdown.shape[1:])
+            down_rs[p].one.start()
         each(backward, c, True)
         mlp_wire.arrived()
         for i in range(rows):
             at = slice(i * blk, (i + 1) * blk)
             out_s[i] = (mid[at, :] + mine[at, :] + xr[2, at, :].astype(F4) + vecs[5:6, :]).astype(BF)
         start_all(out_wires)
-        cot_mate.arrived()
-
-        for p in order:
-            got = dot_tn(act[:, p * hid:(p + 1) * hid], flat(cot[...]))
-            gdown[p] = got.astype(BF).reshape(gdown.shape[1:])
-            down_rs[p].one.start()
         each(backward, cn, False)
         back_wire.start()
         for p in order:
@@ -1251,17 +1251,16 @@
             back_block(j)
             if j == 1:
                 down_rs[3].run(1)
+                up_rs[1].run(1)
+            if j == 2:
                 up_rs[2].run(1)
-            if j == 2:
-                down_rs[0].run(1)
-                up_rs[3].run(1)
                 down_rs[1].run(2)
                 down_rs[2].run(2)
             if j == 3:
-                up_rs[1].run(1)
+                down_rs[0].run(1)
+                up_rs[3].run(1)
                 down_rs[3].run(2)
-                up_rs[2].run(2)
-                up_rs[3].run(2)
+                up_rs[1].run(2)
 
         gq[...] = gqt[...].T
         gk_low = gk[...].astype(BF)
@@ -1276,8 +1275,6 @@
         for wire in gfirst_wires:
             wire.start()
         gfirst_own.start()
-        up_rs[0].run(1)
-        down_rs[0].run(2)
         small[0, 7:8, lanes_h] = jnp.sum(gq[...].astype(F4), axis=0, keepdims=True)
 
         @pl.when(lead)
@@ -1287,8 +1284,6 @@
             small[0, 6:7, :heads_width] = jnp.sum(gv_low.astype(F4), axis=0, keepdims=True)
 
         fresh_reduce(0)
-        heads_out.run(0.5)
-        small_sums[1].run(1)
 
         def back_rows(h, i):
             at = half_rows(h, i)
@@ -1313,7 +1308,12 @@
         lax.fori_loop(0, per_half, back_mate, 0)
         back1_wire.start()
         lax.fori_loop(0, per_half, back_mine, 0)
-        up_rs[1].run(2)
+        up_rs[0].run(1)
+        up_rs[2].run(2)
+        heads_out.run(0.5)
+        small_sums[1].run(1)
+        up_rs[3].run(2)
+        down_rs[0].run(2)
 
     lanes_h = pl.ds(pl.multiple_of(c * heads_width, 128), heads_width)
     pl.run_scoped(
@@ -1343,7 +1343,6 @@
         out_s[i] = (mid[at, :] + norm_back(back, unit, inverse, vecs[0:1, :])).astype(BF)
     small[0, 0:1, :] = gain_sum
     small[0, 1:2, :] = bias_sum
-    start_all(gtok_wires)
     small_sums[0].run(0)
 
     heads_out.run(1)
@@ -1355,6 +1354,7 @@
     small_sums[0].run(1)
     heads_q.run(1)
     heads_k.run(1)
+    start_all(gtok_wires)
     heads_out.run(2)
     up_end.run(0)
     down_end.run(1)

time: 228 us -> 225 us (0.987)
  Pallas kernels: 225 us -> 221 us
    pallas_call x1, Pallas kernels: 218 us -> 214 us  [whole_layer(): pl.pallas_call(layer_kernel, out_shape=outs, in_specs=[hbm, hbm, hbm, vme...]
where the time goes in v4:
time: 225 us; the launch traced here: 222 us
  Pallas kernels  221 us (98%)
    pallas_call x1, Pallas kernels, whole_layer(): pl.pallas_call(layer_kernel, out_shape=outs, in_specs=[hbm, hbm, hbm, vme...  214 us
    pallas_call x1, Pallas kernels, whole_layer(): pl.pallas_call(finish_kernel, out_shape=(of(rows, blk, width), of(rows, b...  6.89 us

profile of v4, /device:TPU:1, one launch (start us, length us, event | category | flops | bytes accessed | tf_op | source)
XLA Modules:
  0.0 222.1 jit_solution(11226263889371366271)
XLA Ops:
  0.7 214.1 %shard_map.322 = (bf16[4,128,768]{2,1,0:T(8,128)(2,1)}, bf16[4,128,768]{2,1,0:T(8,128)(2,1)}, bf16[4,128,384]{2,1,0:T(8,128)(2,1)}, bf16[2,2,192,768]{3,2,1,0:T(...) custom-call(bf16[4,128,768]{2,1,0:T(8,128)(2,1)} %tokens.1, ...), custom_call_target="tpu_custom_call" | custom-call | tf_op jit(solution)/shard_map/pallas_call | solution.py:1442
  214.8 6.9 %shard_map.323 = (bf16[4,128,768]{2,1,0:T(8,128)(2,1)}, bf16[4,128,384]{2,1,0:T(8,128)(2,1)}, f32[4,128,768]{2,1,0:T(8,128)}, f32[768,768]{1,0:T(8,128)}, f32[76...) custom-call(bf16[4,128,768]{2,1,0:T(8,128)(2,1)} %get-tuple-element., ...), custom_call_target="tpu_custom_call" | custom-call | tf_op jit(solution)/shard_map/pallas_call | solution.py:1457

commit v5 on v4

--- a/solution.py
+++ b/solution.py
@@ -1343,6 +1343,7 @@
         out_s[i] = (mid[at, :] + norm_back(back, unit, inverse, vecs[0:1, :])).astype(BF)
     small[0, 0:1, :] = gain_sum
     small[0, 1:2, :] = bias_sum
+    start_all(gtok_wires[:2])
     small_sums[0].run(0)
 
     heads_out.run(1)
@@ -1354,7 +1355,7 @@
     small_sums[0].run(1)
     heads_q.run(1)
     heads_k.run(1)
-    start_all(gtok_wires)
+    start_all(gtok_wires[2:])
     heads_out.run(2)
     up_end.run(0)
     down_end.run(1)

time: 225 us -> 227 us (level)
  the two profiles are of different devices: /device:TPU:1 before, /device:TPU:31 now
where the time goes in v5:
time: 227 us; the launch traced here: 224 us
  Pallas kernels  223 us (98%)
    pallas_call x1, Pallas kernels, whole_layer(): pl.pallas_call(layer_kernel, out_shape=outs, in_specs=[hbm, hbm, hbm, vme...  216 us
    pallas_call x1, Pallas kernels, whole_layer(): pl.pallas_call(finish_kernel, out_shape=(of(rows, blk, width), of(rows, b...  6.89 us

profile of v5, /device:TPU:31, one launch (start us, length us, event | category | flops | bytes accessed | tf_op | source)
XLA Modules:
  0.0 224.4 jit_solution(1041337325901979082)
XLA Ops:
  0.7 216.3 %shard_map.322 = (bf16[4,128,768]{2,1,0:T(8,128)(2,1)}, bf16[4,128,768]{2,1,0:T(8,128)(2,1)}, bf16[4,128,384]{2,1,0:T(8,128)(2,1)}, bf16[2,2,192,768]{3,2,1,0:T(...) custom-call(bf16[4,128,768]{2,1,0:T(8,128)(2,1)} %tokens.1, ...), custom_call_target="tpu_custom_call" | custom-call | tf_op jit(solution)/shard_map/pallas_call | solution.py:1443
  217.0 6.9 %shard_map.323 = (bf16[4,128,768]{2,1,0:T(8,128)(2,1)}, bf16[4,128,384]{2,1,0:T(8,128)(2,1)}, f32[4,128,768]{2,1,0:T(8,128)}, f32[768,768]{1,0:T(8,128)}, f32[76...) custom-call(bf16[4,128,768]{2,1,0:T(8,128)(2,1)} %get-tuple-element., ...), custom_call_target="tpu_custom_call" | custom-call | tf_op jit(solution)/shard_map/pallas_call | solution.py:1458
